TPU v7x, 32 devices: a whole 2x2x4 slice. The times are simulated.
32 devices in a mesh: section: 4 (over x, core), seq: 8 (over z, y).
Axes of the slice: x: 2, y: 2, z: 4, core: 2. Of those that a mesh axis runs over, the one named last changes fastest.
Arguments:
- activations: bfloat16 [4, 2048, 1536], P('section', 'seq'), may hold values from -6 to 6
- qkv_weight: bfloat16 [4, 1536, 4608], P('section'), may hold values from -5 to 5
- out_weight: bfloat16 [4, 1536, 1536], P('section'), may hold values from -0.15625 to 0.15625
- modulation: float32 [4, 3, 1536], P('section'), may hold values from -4 to 4
- key_blocks: int32 [16, 4], replicated, may hold values from 0 to 15, as said below
- block_counts: int32 [16], replicated, may hold values from 3 to 4, as said below
Outputs:
- advanced: bfloat16 [4, 2048, 1536], P('section', 'seq')
Inputs may be any that keep to these rules, and one draw needn't show every extreme that they name: Block b belongs to group b // 2. Row b of key_blocks names first its own block, then the other blocks of its group, then 2 blocks of different groups g with 1 <= |g - b // 2| <= 2. All rows of one group name at most one block of any other group. `block_counts`: some query block uses all 4 entries.
All inputs are finite; a program needn't handle non-finite values.
Results may differ from a plain program's by a relative error of at most 0.008.
Values may be sent and summed in bfloat16 or wider, within the bound.
No kernel may reach another device: no remote copies, remote signals or barrier semaphores. Data moves between devices by JAX's collectives and lax.ppermute only.
A program may use at most 128 MiB of HBM per device.

v0:
```python
import jax
import jax.numpy as jnp
from jax import lax
from jax.sharding import PartitionSpec as P

HEADS = 12
HD = 128
BLK = 128


EPSILON = 1e-06


def from_behind(value, axis, steps):
    count = lax.axis_size(axis)
    first, last = (max(0, -steps), min(count, count - steps))
    return lax.ppermute(value, axis, [(source, source + steps) for source in range(first, last)])


def shifted(block, axis, distance):
    devices = range(lax.axis_size(axis))
    route = [((i - distance) % len(devices), i) for i in devices]
    return lax.ppermute(block, axis, route)


def modulated_norm(tokens_in, segment_mod):
    values = tokens_in.astype(jnp.float32)
    center = jnp.mean(values, axis=-1, keepdims=True)
    spread = jnp.mean(jnp.square(values - center), axis=-1, keepdims=True)
    normed = (values - center) * lax.rsqrt(spread + EPSILON)
    return (normed * (1.0 + segment_mod[1]) + segment_mod[0]).astype(jnp.bfloat16)


def owner_tables(key_blocks, seq_count, blocks_here):
    grouped = key_blocks.reshape(seq_count, blocks_here * key_blocks.shape[1])
    owners = grouped // blocks_here
    device_range = jnp.arange(seq_count, dtype=jnp.int32)
    matches = owners[:, :, None] == device_range[None, None, :]
    chosen = jnp.max(jnp.where(matches, (grouped % blocks_here)[:, :, None], 0), axis=1)
    listed = jnp.any(matches, axis=1)
    return (chosen, listed)


def source_id(source, own_chosen, own_listed, seq_count, blocks_here):
    inside = (source >= 0) & (source < seq_count)
    safe = jnp.clip(source, 0, seq_count - 1)
    return jnp.where(inside & own_listed[safe], safe * blocks_here + own_chosen[safe], -1)


def fetch_blocks(local_blocks, key_blocks, own_index):
    seq_count = lax.axis_size("seq")
    blocks_here = local_blocks.shape[0]
    chosen, listed = owner_tables(key_blocks, seq_count, blocks_here)
    own_chosen = lax.dynamic_index_in_dim(chosen, own_index, 0, keepdims=False)
    own_listed = lax.dynamic_index_in_dim(listed, own_index, 0, keepdims=False)
    asked_of_me = lax.dynamic_index_in_dim(chosen, own_index, 1, keepdims=False)
    arrived = []
    arrived_ids = []
    for distance in (1, -1, 2, -2):
        target = jnp.clip(own_index + distance, 0, seq_count - 1)
        incoming = from_behind(
            lax.dynamic_index_in_dim(local_blocks, asked_of_me[target], 0, keepdims=False),
            "seq",
            distance,
        )
        arrived.append(incoming)
        arrived_ids.append(
            source_id(own_index - distance, own_chosen, own_listed, seq_count, blocks_here)
        )
    own_ids = own_index * blocks_here + jnp.arange(blocks_here, dtype=jnp.int32)
    store = jnp.concatenate([local_blocks, jnp.stack(arrived)], axis=0)
    store_ids = jnp.concatenate([own_ids, jnp.stack(arrived_ids)])
    return (store, store_ids)


def attention_output(tokens_in, weights_in, segment_mod, key_blocks, block_counts, own_index):
    token_count = tokens_in.shape[0]
    inner_width = HEADS * HD
    blocks_here = token_count // BLK
    list_width = key_blocks.shape[1]
    modulated = modulated_norm(tokens_in, segment_mod)
    projected = jnp.dot(modulated, weights_in, preferred_element_type=jnp.float32).astype(
        jnp.bfloat16
    )
    queries = projected[:, :inner_width].reshape(blocks_here, BLK, HEADS, HD)
    local_blocks = projected[:, inner_width:].reshape(blocks_here, BLK, 2 * inner_width)
    store, store_ids = fetch_blocks(local_blocks, key_blocks, own_index)
    rows_here = lax.dynamic_slice_in_dim(key_blocks, own_index * blocks_here, blocks_here, 0)
    counts_here = lax.dynamic_slice_in_dim(block_counts, own_index * blocks_here, blocks_here, 0)
    slot_range = jnp.arange(store_ids.shape[0], dtype=jnp.int32)
    slots = jnp.sum(
        jnp.where(rows_here[:, :, None] == store_ids[None, None, :], slot_range[None, None, :], 0),
        axis=-1,
    )
    picked = jnp.take(store, slots.reshape(-1), axis=0).reshape(
        blocks_here, list_width * BLK, 2 * inner_width
    )
    key_part = picked[:, :, :inner_width].reshape(blocks_here, list_width * BLK, HEADS, HD)
    value_part = picked[:, :, inner_width:].reshape(blocks_here, list_width * BLK, HEADS, HD)
    scores = jnp.einsum(
        "bqhd,bkhd->bhqk", queries, key_part, preferred_element_type=jnp.float32
    ) * HD ** (-0.5)
    live = jnp.repeat(
        jnp.arange(list_width, dtype=jnp.int32)[None, :] < counts_here[:, None], BLK, axis=1
    )
    scores = jnp.where(live[:, None, None, :], scores, -jnp.inf)
    row_peak = jnp.max(scores, axis=-1, keepdims=True)
    exponent = jnp.exp(scores - row_peak)
    denominator = jnp.sum(exponent, axis=-1, keepdims=True)
    weighted = jnp.einsum(
        "bhqk,bkhd->bqhd",
        exponent.astype(jnp.bfloat16),
        value_part,
        preferred_element_type=jnp.float32,
    )
    attended = weighted / jnp.moveaxis(denominator, 1, 2)
    return attended.reshape(token_count, inner_width).astype(jnp.bfloat16)


def finish(tokens_in, attended, weights_out, gate_row):
    output = jnp.dot(attended, weights_out, preferred_element_type=jnp.float32)
    return (tokens_in.astype(jnp.float32) + gate_row * output).astype(jnp.bfloat16)


def on_device(activations, qkv_weight, out_weight, modulation, key_blocks, block_counts):
    own_index = lax.axis_index("seq")
    tokens_in = activations[0]
    weights_in = qkv_weight[0]
    weights_out = out_weight[0]
    segment_mod = modulation[0]
    attended = attention_output(
        tokens_in, weights_in, segment_mod, key_blocks, block_counts, own_index
    )
    handed_over = shifted(finish(tokens_in, attended, weights_out, segment_mod[2]), "section", 1)
    second_attended = attention_output(
        handed_over, weights_in, segment_mod, key_blocks, block_counts, own_index
    )
    return finish(handed_over, second_attended, weights_out, segment_mod[2])[None]


def solution(mesh):
    return jax.shard_map(
        on_device,
        mesh=mesh,
        in_specs=(
            P("section", "seq", None),
            P("section", None, None),
            P("section", None, None),
            P("section", None, None),
            P(),
            P(),
        ),
        out_specs=P("section", "seq", None),
        check_vma=False,
    )
```

profile of v0, /device:TPU:8, one launch (start us, length us, event | category | flops | bytes accessed | tf_op | source)
XLA Modules:
  0.0 197.5 jit_solution(14043744290365623317)
XLA Ops:
  6.7 1.3 convert_reduce_fusion.1
  8.0 1.5 fusion.61
  10.3 9.2 %fusion.4 = bf16[256,4608]{1,0:T(8,128)(2,1)S(1)} fusion(bf16[1,1536,4608]{2,1,0:T(8,128)(2,1)} %param.9, bf16[1,256,1536]{2,1,0:T(8,128)(2,1)} %param.8, f32[1536]{0:T(1024)S(1)} %get-tuple-element.7, f32[1536]{0:T(1024)S(1)} %get-tuple-element.8, f32[256]{0:T(256)S(1)} %add_rsqrt_fusion.1, f32[256]{0:T(256)S(1)} %broadcast_multiply_fusion.1), kind=kOutput, calls=%fused_computation.6 | convolution fusion | flops 3627417600 | bytes 17315840 | tf_op jit(solution)/shard_map/dot_general | solution.py:82
  19.5 1.4 copy-done
  23.7 1.7 dynamic-slice_bitcast_fusion.4
  25.4 1.9 collective-permute-start.3
  27.4 3.9 %collective-permute-start.2 = (bf16[128,3072]{1,0:T(8,128)(2,1)}, bf16[128,3072]{1,0:T(8,128)(2,1)}, u32[]{:S(2)}, u32[]{:S(2)}) collective-permute-start(bf16[128,3072]{1,0:T(8,128)(2,1)} %get-tuple-element.18), channel_id=1, source_target_pairs={{0,2},{1,3},{2,4},{3,5},{4,6},{5,7},{8,10},{9,11},{10,12},{11,13},... | collective-permute-start | bytes 2359304 | tf_op jit(solution)/shard_map/ppermute | solution.py:17
  31.3 4.2 %collective-permute-start.1 = (bf16[128,3072]{1,0:T(8,128)(2,1)}, bf16[128,3072]{1,0:T(8,128)(2,1)}, u32[]{:S(2)}, u32[]{:S(2)}) collective-permute-start(bf16[128,3072]{1,0:T(8,128)(2,1)} %get-tuple-element.19), channel_id=1, source_target_pairs={{1,0},{2,1},{3,2},{4,3},{5,4},{6,5},{7,6},{9,8},{10,9},{11,10},{12... | collective-permute-start | bytes 2359304 | tf_op jit(solution)/shard_map/ppermute | solution.py:17
  35.5 2.1 %collective-permute-start = (bf16[128,3072]{1,0:T(8,128)(2,1)}, bf16[128,3072]{1,0:T(8,128)(2,1)}, u32[]{:S(2)}, u32[]{:S(2)}) collective-permute-start(bf16[128,3072]{1,0:T(8,128)(2,1)} %get-tuple-element.20), channel_id=1, source_target_pairs={{0,1},{1,2},{2,3},{3,4},{4,5},{5,6},{6,7},{8,9},{9,10},{10,11},{11... | collective-permute-start | bytes 2359304 | tf_op jit(solution)/shard_map/ppermute | solution.py:17
  44.1 1.5 reshape.225
  45.6 1.2 constant_dynamic-update-slice_fusion
  46.9 23.9 %collective-permute-done = bf16[128,3072]{1,0:T(8,128)(2,1)} collective-permute-done((bf16[128,3072]{1,0:T(8,128)(2,1)}, bf16[128,3072]{1,0:T(8,128)(2,1)}, u32[]{:S(2)}, u32[]{:S(2)}) %collective-permute-start) | collective-permute-done | bytes 786464 | tf_op jit(solution)/shard_map/ppermute | solution.py:17
  70.8 2.1 %bitcast_dynamic-update-slice_fusion.7 = bf16[6,128,3072]{2,1,0:T(8,128)(2,1)} fusion(bf16[6,128,3072]{2,1,0:T(8,128)(2,1)} %constant_dynamic-update-slice_fusion, bf16[128,3072]{1,0:T(8,128)(2,1)} %collective-permute-done), kind=kLoop, calls=%fused_computation.79 | loop fusion | bytes 1572864
  73.0 2.2 %bitcast_dynamic-update-slice_fusion.6 = bf16[6,128,3072]{2,1,0:T(8,128)(2,1)} fusion(bf16[6,128,3072]{2,1,0:T(8,128)(2,1)} %bitcast_dynamic-update-slice_fusion.7, bf16[128,3072]{1,0:T(8,128)(2,1)} %collective-permute-done.1), kind=kLoop, calls=%fused_computation.78 | loop fusion | bytes 1572864
  75.1 2.1 %bitcast_dynamic-update-slice_fusion.5 = bf16[6,128,3072]{2,1,0:T(8,128)(2,1)} fusion(bf16[6,128,3072]{2,1,0:T(8,128)(2,1)} %bitcast_dynamic-update-slice_fusion.6, bf16[128,3072]{1,0:T(8,128)(2,1)} %collective-permute-done.2), kind=kLoop, calls=%fused_computation.77 | loop fusion | bytes 1572864
  77.2 1.0 bitcast_dynamic-update-slice_fusion.4
  78.1 5.9 %gather_fusion = bf16[8,128,3072]{2,1,0:T(8,128)(2,1)} fusion(bf16[6,128,3072]{2,1,0:T(8,128)(2,1)} %bitcast_dynamic-update-slice_fusion.4, s32[1024]{0:T(1024)S(1)} %pad_clamp_fusion), kind=kCustom, calls=%fused_computation.clone | custom fusion | bytes 12582944 | tf_op jit(solution)/shard_map/jit(_take)/gather | solution.py:95
  84.1 3.5 %broadcast_select_fusion.1 = bf16[8,128,3072]{2,1,0:T(8,128)(2,1)S(1)} fusion(bf16[8,128,3072]{2,1,0:T(8,128)(2,1)} %gather_fusion, pred[8]{0:T(512)(128)(4,1)S(1)} %compare_and_fusion), kind=kLoop, calls=%fused_computation.13 | loop fusion | flops 3145728 | bytes 12582920 | tf_op jit(solution)/shard_map/jit(_take)/select_n | solution.py:95
  87.5 3.2 %fusion.99 = (bf16[2,512,1536]{2,1,0:T(8,128)(2,1)}, bf16[2,512,1536]{2,1,0:T(8,128)(2,1)}) fusion(bf16[2,512,3072]{2,1,0:T(8,128)(2,1)S(1)} %bitcast.141), kind=kLoop, calls=%fused_computation.130 | loop fusion | bytes 12582912 | tf_op jit(solution)/shard_map/slice | solution.py:98
  90.7 3.2 %copy.41 = bf16[2,512,1536]{1,2,0:T(8,128)(2,1)S(1)} copy(bf16[2,512,1536]{2,1,0:T(8,128)(2,1)} %get-tuple-element.11) | data formatting | bytes 6291456 | tf_op jit(solution)/shard_map/slice | solution.py:98
  93.9 4.7 %copy.39 = bf16[2,512,1536]{1,2,0:T(8,128)(2,1)} copy(bf16[2,512,1536]{2,1,0:T(8,128)(2,1)} %get-tuple-element.12) | data formatting | bytes 6291456 | tf_op jit(solution)/shard_map/slice | solution.py:99
  98.6 2.4 %fusion.10 = (f32[2,12,128]{2,1,0:T(8,128)S(1)}, f32[2,12,128,512]{3,2,1,0:T(8,128)S(1)}) fusion(pred[2,512]{1,0:T(4,128)(4,1)S(1)} %bitcast.152, bf16[2,512,12,128]{1,3,2,0:T(8,128)(2,1)S(1)} %bitcast.146, bf16[2,128,12,128]{3,2,1,0:T(8,128)(2,1)} %reshape.225), kind=kOutput, calls=%fused_computation.14 | convolution fusion | flops 407368704 | bytes 10236928 | tf_op jit(solution)/shard_map/bqhd,bkhd->bhqk/dot_general | solution.py:100
  101.0 1.7 fusion.12
  102.9 1.9 fusion.67
  105.7 1.4 fusion.44
  107.1 11.4 %collective-permute-done.4 = bf16[256,1536]{1,0:T(8,128)(2,1)S(1)} collective-permute-done((bf16[256,1536]{1,0:T(8,128)(2,1)S(1)}, bf16[256,1536]{1,0:T(8,128)(2,1)S(1)}, u32[]{:S(2)}, u32[]{:S(2)}) %collective-permute-start.4) | collective-permute-done | bytes 786464 | tf_op jit(solution)/shard_map/ppermute | solution.py:23
  119.2 4.5 %fusion.7 = bf16[256,4608]{1,0:T(8,128)(2,1)S(1)} fusion(bf16[1,1536,4608]{2,1,0:T(8,128)(2,1)S(1)} %bitcast.161, bf16[256,1536]{1,0:T(8,128)(2,1)S(1)} %collective-permute-done.4, f32[1536]{0:T(1024)S(1)} %get-tuple-element.7, f32[1536]{0:T(1024)S(1)} %get-tuple-element.8, f32[256]{0:T(256)S(1)} %add_rsqrt_fusion, f32[256]{0:T(256)S(1)} %broadcast_multiply_fusion), kind=kOutput, calls=%fused_computation.7 | convolution fusion | flops 3627417600 | bytes 17315840 | tf_op jit(solution)/shard_map/dot_general | solution.py:82
  123.8 1.5 dynamic-slice_bitcast_fusion
  125.3 4.4 %collective-permute-start.5 = (bf16[128,3072]{1,0:T(8,128)(2,1)}, bf16[128,3072]{1,0:T(8,128)(2,1)S(1)}, u32[]{:S(2)}, u32[]{:S(2)}) collective-permute-start(bf16[128,3072]{1,0:T(8,128)(2,1)} %get-tuple-element.16), channel_id=1, source_target_pairs={{0,1},{1,2},{2,3},{3,4},{4,5},{5,6},{6,7},{8,9},{9,10},{10,11},{11... | collective-permute-start | bytes 2359304 | tf_op jit(solution)/shard_map/ppermute | solution.py:17
  129.7 2.4 %collective-permute-start.6 = (bf16[128,3072]{1,0:T(8,128)(2,1)}, bf16[128,3072]{1,0:T(8,128)(2,1)S(1)}, u32[]{:S(2)}, u32[]{:S(2)}) collective-permute-start(bf16[128,3072]{1,0:T(8,128)(2,1)} %get-tuple-element.15), channel_id=1, source_target_pairs={{1,0},{2,1},{3,2},{4,3},{5,4},{6,5},{7,6},{9,8},{10,9},{11,10},{12... | collective-permute-start | bytes 2359304 | tf_op jit(solution)/shard_map/ppermute | solution.py:17
  132.1 1.2 constant_dynamic-update-slice_fusion.1
  133.4 1.5 reshape.226
  134.9 1.9 collective-permute-start.8
  136.8 4.1 %collective-permute-start.7 = (bf16[128,3072]{1,0:T(8,128)(2,1)}, bf16[128,3072]{1,0:T(8,128)(2,1)S(1)}, u32[]{:S(2)}, u32[]{:S(2)}) collective-permute-start(bf16[128,3072]{1,0:T(8,128)(2,1)} %get-tuple-element.14), channel_id=1, source_target_pairs={{0,2},{1,3},{2,4},{3,5},{4,6},{5,7},{8,10},{9,11},{10,12},{11,13},... | collective-permute-start | bytes 2359304 | tf_op jit(solution)/shard_map/ppermute | solution.py:17
  140.9 22.0 %collective-permute-done.5 = bf16[128,3072]{1,0:T(8,128)(2,1)S(1)} collective-permute-done((bf16[128,3072]{1,0:T(8,128)(2,1)}, bf16[128,3072]{1,0:T(8,128)(2,1)S(1)}, u32[]{:S(2)}, u32[]{:S(2)}) %collective-permute-start.5) | collective-permute-done | bytes 786464 | tf_op jit(solution)/shard_map/ppermute | solution.py:17
  162.9 1.0 bitcast_dynamic-update-slice_fusion.3
  164.0 1.0 bitcast_dynamic-update-slice_fusion.2
  165.0 0.9 bitcast_dynamic-update-slice_fusion.1
  166.7 1.0 bitcast_dynamic-update-slice_fusion
  167.7 5.9 %gather_fusion.1 = bf16[8,128,3072]{2,1,0:T(8,128)(2,1)} fusion(bf16[6,128,3072]{2,1,0:T(8,128)(2,1)} %bitcast_dynamic-update-slice_fusion, s32[1024]{0:T(1024)S(1)} %pad_clamp_fusion), kind=kCustom, calls=%fused_computation.1.clone | custom fusion | bytes 12582944 | tf_op jit(solution)/shard_map/jit(_take)/gather | solution.py:95
  173.6 3.5 %broadcast_select_fusion = bf16[8,128,3072]{2,1,0:T(8,128)(2,1)S(1)} fusion(bf16[8,128,3072]{2,1,0:T(8,128)(2,1)} %gather_fusion.1, pred[8]{0:T(512)(128)(4,1)S(1)} %compare_and_fusion), kind=kLoop, calls=%fused_computation.12 | loop fusion | flops 3145728 | bytes 12582920 | tf_op jit(solution)/shard_map/jit(_take)/select_n | solution.py:95
  177.1 3.2 %fusion.98 = (bf16[2,512,1536]{2,1,0:T(8,128)(2,1)}, bf16[2,512,1536]{2,1,0:T(8,128)(2,1)}) fusion(bf16[2,512,3072]{2,1,0:T(8,128)(2,1)S(1)} %bitcast.140), kind=kLoop, calls=%fused_computation.129 | loop fusion | bytes 12582912 | tf_op jit(solution)/shard_map/slice | solution.py:98
  180.2 3.2 %copy.47 = bf16[2,512,1536]{1,2,0:T(8,128)(2,1)S(1)} copy(bf16[2,512,1536]{2,1,0:T(8,128)(2,1)} %get-tuple-element.9) | data formatting | bytes 6291456 | tf_op jit(solution)/shard_map/slice | solution.py:98
  183.4 4.7 %copy.45 = bf16[2,512,1536]{1,2,0:T(8,128)(2,1)} copy(bf16[2,512,1536]{2,1,0:T(8,128)(2,1)} %get-tuple-element.10) | data formatting | bytes 6291456 | tf_op jit(solution)/shard_map/slice | solution.py:99
  188.1 2.4 %fusion.11 = (f32[2,12,128]{2,1,0:T(8,128)S(1)}, f32[2,12,128,512]{3,2,1,0:T(8,128)S(1)}) fusion(pred[2,512]{1,0:T(4,128)(4,1)S(1)} %bitcast.155, bf16[2,512,12,128]{1,3,2,0:T(8,128)(2,1)S(1)} %bitcast.147, bf16[2,128,12,128]{3,2,1,0:T(8,128)(2,1)} %reshape.226), kind=kOutput, calls=%fused_computation.15 | convolution fusion | flops 407368704 | bytes 10236928 | tf_op jit(solution)/shard_map/bqhd,bkhd->bhqk/dot_general | solution.py:100
  190.5 1.7 fusion.14
  192.4 1.9 fusion.66
  195.2 2.3 %fusion.50 = bf16[1,256,1536]{2,1,0:T(8,128)(2,1)} fusion(bf16[1,1536,1536]{2,1,0:T(8,128)(2,1)S(1)} %bitcast.165, bf16[256,1536]{1,0:T(8,128)(2,1)S(1)} %copy-done.5, bf16[192,8,2,128]{3,2,1,0:T(2,128)(2,1)S(1)} %bitcast.150, f32[1536]{0:T(1024)S(1)} %get-tuple-element.6), kind=kOutput, calls=%fused_computation.40 | convolution fusion | flops 1209532416 | bytes 7084032 | tf_op jit(solution)/shard_map/dot_general | solution.py:121
  (75 shorter events, 7.8 us)
Async XLA Ops:
  19.5 1.4 copy-start
  20.9 16.8 %copy-start.6 = (s32[16,4]{0,1:T(4,128)S(1)}, s32[16,4]{0,1:T(4,128)}, u32[]{:S(2)}) copy-start(s32[16,4]{0,1:T(4,128)} %param.12) | copy-start | bytes 772
  20.9 16.9 %copy-start.7 = (s32[16]{0:T(128)S(1)}, s32[16]{0:T(128)}, u32[]{:S(2)}) copy-start(s32[16]{0:T(128)} %param.13) | copy-start | bytes 196
  21.1 23.0 %slice-start = ((bf16[256,4608]{1,0:T(8,128)(2,1)}), bf16[256,1536]{1,0:T(8,128)(2,1)S(1)}, s32[]{:S(2)}) async-start(bf16[256,4608]{1,0:T(8,128)(2,1)} %copy-done), calls=%async_computation | async-start | bytes 1572864 | tf_op jit(solution)/shard_map/slice | solution.py:85
  25.4 51.7 %collective-permute-start.3 = (bf16[128,3072]{1,0:T(8,128)(2,1)}, bf16[128,3072]{1,0:T(8,128)(2,1)S(1)}, u32[]{:S(2)}, u32[]{:S(2)}) collective-permute-start(bf16[128,3072]{1,0:T(8,128)(2,1)} %get-tuple-element.17), channel_id=1, source_target_pairs={{2,0},{3,1},{4,2},{5,3},{6,4},{7,5},{10,8},{11,9},{12,10},{13,11},... | collective-permute-start | bytes 2359304 | tf_op jit(solution)/shard_map/ppermute | solution.py:17
  27.4 47.8 %collective-permute-start.2 = (bf16[128,3072]{1,0:T(8,128)(2,1)}, bf16[128,3072]{1,0:T(8,128)(2,1)}, u32[]{:S(2)}, u32[]{:S(2)}) collective-permute-start(bf16[128,3072]{1,0:T(8,128)(2,1)} %get-tuple-element.18), channel_id=1, source_target_pairs={{0,2},{1,3},{2,4},{3,5},{4,6},{5,7},{8,10},{9,11},{10,12},{11,13},... | collective-permute-start | bytes 2359304 | tf_op jit(solution)/shard_map/ppermute | solution.py:17
  31.3 41.7 %collective-permute-start.1 = (bf16[128,3072]{1,0:T(8,128)(2,1)}, bf16[128,3072]{1,0:T(8,128)(2,1)}, u32[]{:S(2)}, u32[]{:S(2)}) collective-permute-start(bf16[128,3072]{1,0:T(8,128)(2,1)} %get-tuple-element.19), channel_id=1, source_target_pairs={{1,0},{2,1},{3,2},{4,3},{5,4},{6,5},{7,6},{9,8},{10,9},{11,10},{12... | collective-permute-start | bytes 2359304 | tf_op jit(solution)/shard_map/ppermute | solution.py:17
  35.5 35.3 %collective-permute-start = (bf16[128,3072]{1,0:T(8,128)(2,1)}, bf16[128,3072]{1,0:T(8,128)(2,1)}, u32[]{:S(2)}, u32[]{:S(2)}) collective-permute-start(bf16[128,3072]{1,0:T(8,128)(2,1)} %get-tuple-element.20), channel_id=1, source_target_pairs={{0,1},{1,2},{2,3},{3,4},{4,5},{5,6},{6,7},{8,9},{9,10},{10,11},{11... | collective-permute-start | bytes 2359304 | tf_op jit(solution)/shard_map/ppermute | solution.py:17
  101.0 1.9 copy-start.2
  101.0 4.7 %slice-start.5 = ((s8[4718592]{0:T(1024)(128)(4,1)}), s8[4194304]{0:T(1024)(128)(4,1)S(1)}, s32[]{:S(2)}) async-start(s8[4718592]{0:T(1024)(128)(4,1)} %bitcast.162), calls=%async_computation.5 | async-start | bytes 8388608
  102.8 2.8 %copy-start.3 = (bf16[1,256,1536]{2,1,0:T(8,128)(2,1)S(1)}, bf16[1,256,1536]{2,1,0:T(8,128)(2,1)}, u32[]{:S(2)}) copy-start(bf16[1,256,1536]{2,1,0:T(8,128)(2,1)} %param.8) | copy-start | bytes 2359300
  102.9 2.8 %slice-start.6 = ((s8[4718592]{0:T(1024)(128)(4,1)}), s8[524288]{0:T(1024)(128)(4,1)S(1)}, s32[]{:S(2)}) async-start(s8[4718592]{0:T(1024)(128)(4,1)} %bitcast.162), calls=%async_computation.6 | async-start | bytes 1048576
  102.9 16.2 %slice-start.1 = ((s8[14155776]{0:T(1024)(128)(4,1)}), s8[1572864]{0:T(1024)(128)(4,1)S(1)}, s32[]{:S(2)}) async-start(s8[14155776]{0:T(1024)(128)(4,1)} %bitcast.160), calls=%async_computation.1 | async-start | bytes 3145728
  102.9 16.3 %slice-start.2 = ((s8[14155776]{0:T(1024)(128)(4,1)}), s8[4194304]{0:T(1024)(128)(4,1)S(1)}, s32[]{:S(2)}) async-start(s8[14155776]{0:T(1024)(128)(4,1)} %bitcast.160), calls=%async_computation.2 | async-start | bytes 8388608
  102.9 16.3 %slice-start.3 = ((s8[14155776]{0:T(1024)(128)(4,1)}), s8[4194304]{0:T(1024)(128)(4,1)S(1)}, s32[]{:S(2)}) async-start(s8[14155776]{0:T(1024)(128)(4,1)} %bitcast.160), calls=%async_computation.3 | async-start | bytes 8388608
  105.7 13.5 %slice-start.4 = ((s8[14155776]{0:T(1024)(128)(4,1)}), s8[4194304]{0:T(1024)(128)(4,1)S(1)}, s32[]{:S(2)}) async-start(s8[14155776]{0:T(1024)(128)(4,1)} %bitcast.160), calls=%async_computation.4 | async-start | bytes 8388608
  107.1 11.5 %collective-permute-start.4 = (bf16[256,1536]{1,0:T(8,128)(2,1)S(1)}, bf16[256,1536]{1,0:T(8,128)(2,1)S(1)}, u32[]{:S(2)}, u32[]{:S(2)}) collective-permute-start(bf16[256,1536]{1,0:T(8,128)(2,1)S(1)} %fusion.44), channel_id=1, source_target_pairs={{24,0},{0,8},{8,16},{16,24},{25,1},{1,9},{9,17},{17,25},{26,2},{2,... | collective-permute-start | bytes 2359304 | tf_op jit(solution)/shard_map/ppermute | solution.py:23
  118.5 5.1 %copy-start.4 = (bf16[256,1536]{1,0:T(8,128)(2,1)}, bf16[256,1536]{1,0:T(8,128)(2,1)S(1)}, u32[]{:S(2)}) copy-start(bf16[256,1536]{1,0:T(8,128)(2,1)S(1)} %collective-permute-done.4) | copy-start | bytes 2359300
  125.3 37.6 %collective-permute-start.5 = (bf16[128,3072]{1,0:T(8,128)(2,1)}, bf16[128,3072]{1,0:T(8,128)(2,1)S(1)}, u32[]{:S(2)}, u32[]{:S(2)}) collective-permute-start(bf16[128,3072]{1,0:T(8,128)(2,1)} %get-tuple-element.16), channel_id=1, source_target_pairs={{0,1},{1,2},{2,3},{3,4},{4,5},{5,6},{6,7},{8,9},{9,10},{10,11},{11... | collective-permute-start | bytes 2359304 | tf_op jit(solution)/shard_map/ppermute | solution.py:17
  129.7 34.3 %collective-permute-start.6 = (bf16[128,3072]{1,0:T(8,128)(2,1)}, bf16[128,3072]{1,0:T(8,128)(2,1)S(1)}, u32[]{:S(2)}, u32[]{:S(2)}) collective-permute-start(bf16[128,3072]{1,0:T(8,128)(2,1)} %get-tuple-element.15), channel_id=1, source_target_pairs={{1,0},{2,1},{3,2},{4,3},{5,4},{6,5},{7,6},{9,8},{10,9},{11,10},{12... | collective-permute-start | bytes 2359304 | tf_op jit(solution)/shard_map/ppermute | solution.py:17
  134.9 31.9 %collective-permute-start.8 = (bf16[128,3072]{1,0:T(8,128)(2,1)S(1)}, bf16[128,3072]{1,0:T(8,128)(2,1)S(1)}, u32[]{:S(2)}, u32[]{:S(2)}) collective-permute-start(bf16[128,3072]{1,0:T(8,128)(2,1)S(1)} %get-tuple-element.13), channel_id=1, source_target_pairs={{2,0},{3,1},{4,2},{5,3},{6,4},{7,5},{10,8},{11,9},{12,10},{13,11},... | collective-permute-start | bytes 2359304 | tf_op jit(solution)/shard_map/ppermute | solution.py:17
  136.8 28.2 %collective-permute-start.7 = (bf16[128,3072]{1,0:T(8,128)(2,1)}, bf16[128,3072]{1,0:T(8,128)(2,1)S(1)}, u32[]{:S(2)}, u32[]{:S(2)}) collective-permute-start(bf16[128,3072]{1,0:T(8,128)(2,1)} %get-tuple-element.14), channel_id=1, source_target_pairs={{0,2},{1,3},{2,4},{3,5},{4,6},{5,7},{8,10},{9,11},{10,12},{11,13},... | collective-permute-start | bytes 2359304 | tf_op jit(solution)/shard_map/ppermute | solution.py:17
  190.5 1.9 copy-start.1
  190.5 4.6 %slice-start.7 = ((s8[4718592]{0:T(1024)(128)(4,1)}), s8[4194304]{0:T(1024)(128)(4,1)S(1)}, s32[]{:S(2)}) async-start(s8[4718592]{0:T(1024)(128)(4,1)} %bitcast.164), calls=%async_computation.7 | async-start | bytes 8388608
  192.4 2.7 %copy-start.5 = (bf16[256,1536]{1,0:T(8,128)(2,1)S(1)}, bf16[256,1536]{1,0:T(8,128)(2,1)}, u32[]{:S(2)}) copy-start(bf16[256,1536]{1,0:T(8,128)(2,1)} %copy-done.4) | copy-start | bytes 2359300
  192.4 2.7 %slice-start.8 = ((s8[4718592]{0:T(1024)(128)(4,1)}), s8[524288]{0:T(1024)(128)(4,1)S(1)}, s32[]{:S(2)}) async-start(s8[4718592]{0:T(1024)(128)(4,1)} %bitcast.164), calls=%async_computation.8 | async-start | bytes 1048576
where the time goes:
time: 200 us; the launch traced here: 197 us
  local copies, waits for them, and re-layouts  60.4 us (30%)
  waiting for transfers between devices  58.1 us (29%)
  matrix products  26 us (13%)
  starting transfers between devices  25 us (12%)
  other arithmetic  14.9 us (7%)
  between operations  13 us (6%)
    ppermute x8, waiting for transfers between devices, from_behind(): lax.ppermute(value, axis, [(source, source + steps) for source in range(f...  46.7 us
    ppermute x8, starting transfers between devices, from_behind(): lax.ppermute(value, axis, [(source, source + steps) for source in range(f...  24.9 us
    unnamed x43, local copies, waits for them, and re-layouts  14.5 us
    dot_general x2, matrix products, attention_output(): jnp.dot(modulated, weights_in, preferred_element_type=jnp.float32)  13.7 us
    slice x4, local copies, waits for them, and re-layouts, attention_output(): picked[:, :, :inner_width].reshape(blocks_here, list_width * BLK, HEADS, HD)  12.7 us
    gather x2, local copies, waits for them, and re-layouts, attention_output(): jnp.take(store, slots.reshape(-1), axis=0)  11.9 us
    ppermute x1, waiting for transfers between devices, shifted(): return lax.ppermute(block, axis, route)  11.4 us
    slice x2, local copies, waits for them, and re-layouts, attention_output(): picked[:, :, inner_width:].reshape(blocks_here, list_width * BLK, HEADS, HD)  9.32 us
  transfers between devices with their start and end apart: 9, of which 4 were waited for; matrix products, arithmetic and copies ran while one was open for 8% of the time, Pallas kernels for 0%

commit v1 on v0

v1 whole, which is shorter than its diff:
```python
import functools

import jax
import jax.numpy as jnp
from jax import lax
from jax.experimental import pallas as pl
from jax.experimental.pallas import tpu as pltpu
from jax.sharding import PartitionSpec as P

HEADS = 12
HD = 128
BLK = 128
EPSILON = 1e-06
INNER = HEADS * HD
PAIR = 2 * HD
TO_EXP2 = HD ** (-0.5) * 1.4426950408889634
MASKED = -1e30
MIB = 2**20

IN_VMEM = pl.BlockSpec(memory_space=pltpu.VMEM)
IN_SMEM = pl.BlockSpec(memory_space=pltpu.SMEM)


def beyond(me, count):
    one = me + 1 - 2 * (me % 2)
    other_one = me - 1 + 2 * (me % 2)
    two = me + 2 - 4 * ((me // 2) % 2)
    other_two = me - 2 + 4 * ((me // 2) % 2)
    return [one, other_one, two, other_two]


def partner_table(count):
    table = []
    for me in range(count):
        table.append([p if 0 <= p < count else me for p in beyond(me, count)])
    return table


def pairs_of(exchange, count):
    table = partner_table(count)
    return [(me, table[me][exchange]) for me in range(count)]


def asked_block(key_ref, target, me, blocks_here):
    width = key_ref.shape[0]
    found = jnp.int32(0)
    for row in range(blocks_here):
        for entry in range(width):
            named = key_ref[entry, target * blocks_here + row]
            mine = (named >= me * blocks_here) & (named < (me + 1) * blocks_here)
            found = jnp.where(mine, named - me * blocks_here, found)
    return found


def partners_here(me, count):
    out = []
    for p in beyond(me, count):
        out.append(jnp.where((p >= 0) & (p < count), p, me))
    return out


def pick_kernel(count, key_ref, x_ref, *rest):
    outs = rest
    me = lax.axis_index("seq")
    blocks_here = x_ref.shape[0] // BLK
    for i, target in enumerate(partners_here(me, count)):
        start = pl.multiple_of(asked_block(key_ref, target, me, blocks_here) * BLK, BLK)
        outs[i][...] = x_ref[pl.ds(start, BLK), :]


def pick_blocks(x, key_blocks, count):
    part = jax.ShapeDtypeStruct((BLK, x.shape[1]), x.dtype)
    return pl.pallas_call(
        functools.partial(pick_kernel, count),
        out_shape=[part] * 4,
        in_specs=[IN_SMEM, IN_VMEM],
        out_specs=[IN_VMEM] * 4,
        name="pick_blocks",
    )(key_blocks, x)


def norm_rows(x_ref, mod_ref, out_ref, out_row):
    rows, width = x_ref.shape
    shift = mod_ref[0]
    scale = 1.0 + mod_ref[1]
    step = 16
    for r in range(0, rows, step):
        values = x_ref[r : r + step, :].astype(jnp.float32)
        center = jnp.sum(values, axis=-1, keepdims=True) * (1.0 / width)
        values = values - center
        spread = jnp.sum(values * values, axis=-1, keepdims=True) * (1.0 / width)
        normed = values * lax.rsqrt(spread + EPSILON)
        out_ref[out_row + r : out_row + r + step, :] = (normed * scale + shift).astype(jnp.bfloat16)


def project(source, weight_ref, column, width):
    return jnp.dot(
        source, weight_ref[:, column : column + width], preferred_element_type=jnp.float32
    ).astype(jnp.bfloat16)


def own_kernel(x_ref, mod_ref, w_ref, qkv_ref, normed):
    norm_rows(x_ref, mod_ref, normed, 0)
    for c in range(0, w_ref.shape[1], 2 * PAIR):
        qkv_ref[:, c : c + 2 * PAIR] = project(normed[...], w_ref, c, 2 * PAIR)


def own_projection(x, mod, w):
    return pl.pallas_call(
        own_kernel,
        out_shape=jax.ShapeDtypeStruct((x.shape[0], w.shape[1]), jnp.bfloat16),
        in_specs=[IN_VMEM] * 3,
        out_specs=IN_VMEM,
        scratch_shapes=[pltpu.VMEM(x.shape, jnp.bfloat16)],
        compiler_params=pltpu.CompilerParams(vmem_limit_bytes=16 * MIB),
        name="own_projection",
    )(x, mod, w)


def early_kernel(a_ref, b_ref, mod_ref, w_ref, kv_ref, normed):
    norm_rows(a_ref, mod_ref, normed, 0)
    norm_rows(b_ref, mod_ref, normed, BLK)
    for c in range(0, 2 * INNER, 2 * PAIR):
        kv_ref[:, c : c + 2 * PAIR] = project(normed[...], w_ref, INNER + c, 2 * PAIR)


def early_projection(a, b, mod, w):
    return pl.pallas_call(
        early_kernel,
        out_shape=jax.ShapeDtypeStruct((2 * BLK, 2 * INNER), jnp.bfloat16),
        in_specs=[IN_VMEM] * 4,
        out_specs=IN_VMEM,
        scratch_shapes=[pltpu.VMEM((2 * BLK, a.shape[1]), jnp.bfloat16)],
        compiler_params=pltpu.CompilerParams(vmem_limit_bytes=16 * MIB),
        name="early_projection",
    )(a, b, mod, w)


def slot_of(named, me, count, blocks_here, order):
    owner = named // blocks_here
    slot = jnp.int32(0)
    for i, p in enumerate(beyond(me, count)):
        slot = jnp.where(owner == p, order.index(i), slot)
    return slot


def tail_kernel(
    count, order, with_sends, key_ref, count_ref, x_ref, qkv_ref, early_ref, c_ref, d_ref, mod_ref, w_ref, wo_ref, *rest
):
    if with_sends:
        y_ref, *sends = rest[:5]
        store, normed, attended = rest[5:]
    else:
        y_ref, sends = rest[0], []
        store, normed, attended = rest[1:]
    me = lax.axis_index("seq")
    tokens = x_ref.shape[0]
    blocks_here = tokens // BLK
    half = 2 * BLK
    norm_rows(c_ref, mod_ref, normed, 0)
    norm_rows(d_ref, mod_ref, normed, BLK)
    remote = key_ref.shape[0] - blocks_here
    starts, alive = [], []
    for i in range(blocks_here):
        row = me * blocks_here + i
        listed = count_ref[row]
        starts.append(
            [
                pl.multiple_of(slot_of(key_ref[blocks_here + j, row], me, count, blocks_here, order) * BLK, BLK)
                for j in range(remote)
            ]
        )
        alive.append([blocks_here + j < listed for j in range(remote)])
    for pair in range(HEADS // 2):
        at = pair * PAIR
        store[0:half, at : at + PAIR] = early_ref[:, at : at + PAIR]
        store[0:half, INNER + at : INNER + at + PAIR] = early_ref[:, INNER + at : INNER + at + PAIR]
        store[half : 2 * half, at : at + PAIR] = project(normed[...], w_ref, INNER + at, PAIR)
        store[half : 2 * half, INNER + at : INNER + at + PAIR] = project(normed[...], w_ref, 2 * INNER + at, PAIR)
        for h in (2 * pair, 2 * pair + 1):
            col = h * HD
            q = qkv_ref[:, col : col + HD]
            k_own = qkv_ref[:, INNER + col : INNER + col + HD]
            v_own = qkv_ref[:, 2 * INNER + col : 2 * INNER + col + HD]
            s_own_all = lax.dot_general(
                q, k_own, (((1,), (1,)), ((), ())), preferred_element_type=jnp.float32
            )
            for i in range(blocks_here):
                rows = slice(i * BLK, (i + 1) * BLK)
                s_own = s_own_all[rows]
                k_far = jnp.concatenate(
                    [store[pl.ds(s, BLK), col : col + HD] for s in starts[i]], axis=0
                )
                v_far = jnp.concatenate(
                    [store[pl.ds(s, BLK), INNER + col : INNER + col + HD] for s in starts[i]], axis=0
                )
                s_far = lax.dot_general(
                    q[rows], k_far, (((1,), (1,)), ((), ())), preferred_element_type=jnp.float32
                )
                far = [
                    jnp.where(alive[i][j], s_far[:, j * BLK : (j + 1) * BLK], MASKED) for j in range(remote)
                ]
                s_all = jnp.concatenate([s_own] + far, axis=1)
                peak = jnp.max(s_all, axis=-1, keepdims=True)
                p = jnp.exp2((s_all - peak) * TO_EXP2)
                total = jnp.sum(p, axis=-1, keepdims=True)
                weighted = jnp.dot(
                    p.astype(jnp.bfloat16),
                    jnp.concatenate([v_own, v_far], axis=0),
                    preferred_element_type=jnp.float32,
                )
                attended[rows, col : col + HD] = (weighted / total).astype(jnp.bfloat16)
    for c in range(0, wo_ref.shape[1], 2 * PAIR):
        cols = slice(c, c + 2 * PAIR)
        out = jnp.dot(attended[...], wo_ref[:, cols], preferred_element_type=jnp.float32)
        y_ref[:, cols] = (x_ref[:, cols].astype(jnp.float32) + mod_ref[2, :, cols] * out).astype(jnp.bfloat16)
    for send, target in zip(sends, partners_here(me, count)):
        start = pl.multiple_of(asked_block(key_ref, target, me, blocks_here) * BLK, BLK)
        send[...] = y_ref[pl.ds(start, BLK), :]


def tail(x, qkv, early, late, mod, w, wo, key_blocks, block_counts, count, order, with_sends):
    part = jax.ShapeDtypeStruct((BLK, x.shape[1]), x.dtype)
    whole = jax.ShapeDtypeStruct(x.shape, x.dtype)
    return pl.pallas_call(
        functools.partial(tail_kernel, count, order, with_sends),
        out_shape=[whole] + [part] * (4 if with_sends else 0),
        in_specs=[IN_SMEM] * 2 + [IN_VMEM] * 8,
        out_specs=[IN_VMEM] * (5 if with_sends else 1),
        scratch_shapes=[
            pltpu.VMEM((4 * BLK, 2 * INNER), jnp.bfloat16),
            pltpu.VMEM((2 * BLK, x.shape[1]), jnp.bfloat16),
            pltpu.VMEM((x.shape[0], INNER), jnp.bfloat16),
        ],
        compiler_params=pltpu.CompilerParams(vmem_limit_bytes=16 * MIB),
        name="tail",
    )(key_blocks, block_counts, x, qkv, early, *late, mod, w, wo)


def on_device(activations, qkv_weight, out_weight, modulation, key_blocks, block_counts):
    count = lax.axis_size("seq")
    sections = lax.axis_size("section")
    x, w, wo = activations[0], qkv_weight[0], out_weight[0]
    mod = modulation.reshape(modulation.shape[1], 1, modulation.shape[2])
    key_blocks = key_blocks.T
    order = [1, 0, 2, 3]

    sends = pick_blocks(x, key_blocks, count)
    got = [lax.ppermute(sends[i], "seq", pairs_of(i, count)) for i in order]
    qkv = own_projection(x, mod, w)
    early = early_projection(got[0], got[1], mod, w)
    y, *sends = tail(
        x, qkv, early, got[2:], mod, w, wo, key_blocks, block_counts, count, order, True
    )

    x2 = lax.ppermute(y, "section", [(s, (s + 1) % sections) for s in range(sections)])
    got = []
    for i in order:
        moved = [
            (s * count + a, (s + 1) % sections * count + b)
            for s in range(sections)
            for a, b in pairs_of(i, count)
        ]
        got.append(lax.ppermute(sends[i], ("section", "seq"), moved))
    qkv = own_projection(x2, mod, w)
    early = early_projection(got[0], got[1], mod, w)
    (out,) = tail(
        x2, qkv, early, got[2:], mod, w, wo, key_blocks, block_counts, count, order, False
    )
    return out[None]


def solution(mesh):
    return jax.shard_map(
        on_device,
        mesh=mesh,
        in_specs=(
            P("section", "seq", None),
            P("section", None, None),
            P("section", None, None),
            P("section", None, None),
            P(),
            P(),
        ),
        out_specs=P("section", "seq", None),
        check_vma=False,
    )
```

time: 200 us -> 90.8 us (0.45); the launches traced: 197 us -> 90.4 us
  local copies, waits for them, and re-layouts: 60.4 us -> 6.91 us
  Pallas kernels: 0 us -> 43.1 us
  waiting for transfers between devices: 58.1 us -> 26.2 us
  matrix products: 26 us -> 0 us
  other arithmetic: 14.9 us -> 0 us
  between operations: 13 us -> 0.19 us
  starting transfers between devices: 25 us -> 14.1 us
    pallas_call x0 -> x7, Pallas kernels: none -> 43.1 us  [the longest x2 25.8 us: tail(): pl.pallas_call(functools.partial(tail_kernel, count, order, with_sends),...]
    ppermute x9, waiting for transfers between devices: 58.1 us -> 26.2 us  [the longest x4 23.7 us: on_device(): got.append(lax.ppermute(sends[i], ('section', 'seq'), moved))]
    dot_general x8 -> x0, matrix products: 26 us -> none  [the longest x2 13.7 us: attention_output(): jnp.dot(modulated, weights_in, preferred_element_type=jnp.float32)]
    slice x11 -> x0, local copies, waits for them, and re-layouts: 22.5 us -> none  [the longest x4 12.7 us: attention_output(): picked[:, :, :inner_width].reshape(blocks_here, list_width * BLK, HEADS, HD)]
    gather x2 -> x0, local copies, waits for them, and re-layouts: 11.9 us -> none  [attention_output(): jnp.take(store, slots.reshape(-1), axis=0)]
    ppermute x9, starting transfers between devices: 25 us -> 14.1 us  [the longest x4 8.49 us: on_device(): got = [lax.ppermute(sends[i], 'seq', pairs_of(i, count)) for i in order]]
    unnamed x43 -> x18, local copies, waits for them, and re-layouts: 14.5 us -> 6.91 us
    select_n x4 -> x0, other arithmetic: 6.92 us -> none  [the longest x3 6.91 us: attention_output(): jnp.take(store, slots.reshape(-1), axis=0)]
  transfers between devices with their start and end apart: 9 -> 9, of which waited for: 4 -> 3; matrix products, arithmetic and copies ran while one was open for 8% -> 0% of each run, Pallas kernels for 0% -> 16%
where the time goes in v1:
time: 90.8 us; the launch traced here: 90.4 us
  Pallas kernels  43.1 us (47%)
  waiting for transfers between devices  26.2 us (29%)
  starting transfers between devices  14.1 us (16%)
  local copies, waits for them, and re-layouts  6.91 us (8%)
    pallas_call x2, Pallas kernels, tail(): pl.pallas_call(functools.partial(tail_kernel, count, order, with_sends),...  25.8 us
    ppermute x4, waiting for transfers between devices, on_device(): got.append(lax.ppermute(sends[i], ('section', 'seq'), moved))  23.7 us
    pallas_call x2, Pallas kernels, own_projection(): pl.pallas_call(own_kernel, out_shape=jax.ShapeDtypeStruct((x.shape[0], w....  8.69 us
    ppermute x4, starting transfers between devices, on_device(): got = [lax.ppermute(sends[i], 'seq', pairs_of(i, count)) for i in order]  8.49 us
    unnamed x18, local copies, waits for them, and re-layouts  6.91 us
    pallas_call x2, Pallas kernels, early_projection(): pl.pallas_call(early_kernel, out_shape=jax.ShapeDtypeStruct((2 * BLK, 2 *...  6.18 us
    ppermute x4, starting transfers between devices, on_device(): got.append(lax.ppermute(sends[i], ('section', 'seq'), moved))  5.49 us
    ppermute x4, waiting for transfers between devices, on_device(): got = [lax.ppermute(sends[i], 'seq', pairs_of(i, count)) for i in order]  2.49 us
  transfers between devices with their start and end apart: 9, of which 3 were waited for; matrix products, arithmetic and copies ran while one was open for 0% of the time, Pallas kernels for 16%

profile of v1, /device:TPU:8, one launch (start us, length us, event | category | flops | bytes accessed | tf_op | source)
XLA Modules:
  0.0 90.4 jit_solution(899087351562866317)
XLA Ops:
  0.0 2.4 %pick_blocks.1 = (bf16[128,1536]{1,0:T(8,128)(2,1)}, bf16[128,1536]{1,0:T(8,128)(2,1)}, bf16[128,1536]{1,0:T(8,128)(2,1)}, bf16[128,1536]{1,0:T(8,128)(2,1)}) custom-call(s32[4,16]{1,0:T(4,128)} %bitcast.23, bf16[256,1536]{1,0:T(8,128)(2,1)} %bitcast.14), custom_call_target="tpu_custom_call" | custom-call | tf_op jit(solution)/shard_map/pick_blocks/pallas_call | solution.py:73
  2.4 3.3 %collective-permute-start = (bf16[128,1536]{1,0:T(8,128)(2,1)}, bf16[128,1536]{1,0:T(8,128)(2,1)S(1)}, u32[]{:S(2)}, u32[]{:S(2)}) collective-permute-start(bf16[128,1536]{1,0:T(8,128)(2,1)} %get-tuple-element.14), channel_id=1, source_target_pairs={{0,0},{1,2},{2,1},{3,4},{4,3},{5,6},{6,5},{7,7},{8,8},{9,10},{10,9... | collective-permute-start | bytes 1179656 | tf_op jit(solution)/shard_map/ppermute | solution.py:249
  5.7 1.7 %collective-permute-start.1 = (bf16[128,1536]{1,0:T(8,128)(2,1)}, bf16[128,1536]{1,0:T(8,128)(2,1)S(1)}, u32[]{:S(2)}, u32[]{:S(2)}) collective-permute-start(bf16[128,1536]{1,0:T(8,128)(2,1)} %get-tuple-element.15), channel_id=1, source_target_pairs={{0,1},{1,0},{2,3},{3,2},{4,5},{5,4},{6,7},{7,6},{8,9},{9,8},{10,11... | collective-permute-start | bytes 1179656 | tf_op jit(solution)/shard_map/ppermute | solution.py:249
  7.4 0.4 collective-permute-start.2
  7.9 3.0 %collective-permute-start.3 = (bf16[128,1536]{1,0:T(8,128)(2,1)}, bf16[128,1536]{1,0:T(8,128)(2,1)S(1)}, u32[]{:S(2)}, u32[]{:S(2)}) collective-permute-start(bf16[128,1536]{1,0:T(8,128)(2,1)} %get-tuple-element.17), channel_id=1, source_target_pairs={{0,0},{1,1},{2,4},{3,5},{4,2},{5,3},{6,6},{7,7},{8,8},{9,9},{10,12... | collective-permute-start | bytes 1179656 | tf_op jit(solution)/shard_map/ppermute | solution.py:249
  10.9 0.0 copy-start
  10.9 5.0 %copy-done = bf16[1,1536,4608]{2,1,0:T(8,128)(2,1)S(1)} copy-done((bf16[1,1536,4608]{2,1,0:T(8,128)(2,1)S(1)}, bf16[1,1536,4608]{2,1,0:T(8,128)(2,1)}, u32[]{:S(2)}) %copy-start) | copy-done | bytes 14155800
  15.9 0.0 copy-start.3
  16.0 1.1 %copy-done.3 = bf16[1,256,1536]{2,1,0:T(8,128)(2,1)S(1)} copy-done((bf16[1,256,1536]{2,1,0:T(8,128)(2,1)S(1)}, bf16[1,256,1536]{2,1,0:T(8,128)(2,1)}, u32[]{:S(2)}) %copy-start.3) | copy-done | bytes 786456
  17.1 0.0 copy-start.5
  17.1 0.7 copy-done.5
  17.8 0.0 copy-start.1
  17.8 4.3 %own_projection.2.qkv_ref = bf16[256,4608]{1,0:T(8,128)(2,1)S(1)} custom-call(bf16[256,1536]{1,0:T(8,128)(2,1)S(1)} %bitcast.15, f32[3,1,1536]{2,1,0:T(1,128)S(1)} %bitcast.17, bf16[1536,4608]{1,0:T(8,128)(2,1)S(1)} %bitcast.6), custom_call_target="tpu_custom_call" | custom-call | tf_op jit(solution)/shard_map/own_projection/pallas_call | solution.py:109
  22.2 0.0 copy-start.4
  22.2 0.0 copy-start.7
  22.2 0.0 copy-start.8
  22.2 0.0 collective-permute-done.a_ref
  22.2 2.5 %collective-permute-done.1.b_ref = bf16[128,1536]{1,0:T(8,128)(2,1)S(1)} collective-permute-done((bf16[128,1536]{1,0:T(8,128)(2,1)}, bf16[128,1536]{1,0:T(8,128)(2,1)S(1)}, u32[]{:S(2)}, u32[]{:S(2)}) %collective-permute-start.1) | collective-permute-done | bytes 393248 | tf_op jit(solution)/shard_map/ppermute | solution.py:249
  24.7 0.0 copy-done.1
  24.7 0.0 copy-start.2
  24.7 3.1 %early_projection.2.early_ref = bf16[256,3072]{1,0:T(8,128)(2,1)S(1)} custom-call(bf16[128,1536]{1,0:T(8,128)(2,1)S(1)} %collective-permute-done.a_ref, bf16[128,1536]{1,0:T(8,128)(2,1)S(1)} %collective-permute-done.1.b_ref, f32[3,1,1536]{2,1,0:T(1,128)S(1)} %bitcast.18, bf16[1536,4608]{1,0:T(8,128)(2,1)S(1)} %bitcast.7), custom_call_target="tpu_custom_call" | custom-call | tf_op jit(solution)/shard_map/early_projection/pallas_call | solution.py:128
  27.8 0.0 collective-permute-done.2.c_ref
  27.8 0.0 collective-permute-done.3.d_ref
  27.8 0.0 copy-done.4
  27.8 0.0 copy-done.7
  27.8 0.0 copy-done.8
  27.8 0.0 copy-done.2
  27.8 0.0 copy-start.6
  27.9 12.6 %tail.2 = (bf16[256,1536]{1,0:T(8,128)(2,1)S(1)}, bf16[128,1536]{1,0:T(8,128)(2,1)S(1)}, bf16[128,1536]{1,0:T(8,128)(2,1)S(1)}, bf16[128,1536]{1,0:T(8,128)(2,1)S(1)}, bf16[128,1536]{1,0:T(8,128)(2,1)S(1)}) custom-call(s32[4,16]{1,0:T(4,128)S(1)} %bitcast.24, s32[16]{0:T(128)S(1)} %copy-done.8, bf16[256,1536]{1,0:T(8,128)(2,1)S(1)} %bitcast.16, ...), custom_call_target="tpu_custom_call" | custom-call | tf_op jit(solution)/shard_map/tail/pallas_call | solution.py:225
  40.5 0.1 collective-permute-start.4
  40.5 2.6 %collective-permute-start.5 = (bf16[128,1536]{1,0:T(8,128)(2,1)S(1)}, bf16[128,1536]{1,0:T(8,128)(2,1)S(1)}, u32[]{:S(2)}, u32[]{:S(2)}) collective-permute-start(bf16[128,1536]{1,0:T(8,128)(2,1)S(1)} %get-tuple-element.19), channel_id=1, source_target_pairs={{0,8},{1,10},{2,9},{3,12},{4,11},{5,14},{6,13},{7,15},{8,16},{9,18... | collective-permute-start | bytes 1179656 | tf_op jit(solution)/shard_map/ppermute | solution.py:264
  43.1 1.1 %collective-permute-start.6 = (bf16[128,1536]{1,0:T(8,128)(2,1)S(1)}, bf16[128,1536]{1,0:T(8,128)(2,1)S(1)}, u32[]{:S(2)}, u32[]{:S(2)}) collective-permute-start(bf16[128,1536]{1,0:T(8,128)(2,1)S(1)} %get-tuple-element.20), channel_id=1, source_target_pairs={{0,9},{1,8},{2,11},{3,10},{4,13},{5,12},{6,15},{7,14},{8,17},{9,16... | collective-permute-start | bytes 1179656 | tf_op jit(solution)/shard_map/ppermute | solution.py:264
  44.3 0.6 collective-permute-start.7
  44.9 1.1 %collective-permute-start.8 = (bf16[128,1536]{1,0:T(8,128)(2,1)S(1)}, bf16[128,1536]{1,0:T(8,128)(2,1)S(1)}, u32[]{:S(2)}, u32[]{:S(2)}) collective-permute-start(bf16[128,1536]{1,0:T(8,128)(2,1)S(1)} %get-tuple-element.22), channel_id=1, source_target_pairs={{0,8},{1,9},{2,12},{3,13},{4,10},{5,11},{6,14},{7,15},{8,16},{9,17... | collective-permute-start | bytes 1179656 | tf_op jit(solution)/shard_map/ppermute | solution.py:264
  46.0 7.4 %collective-permute-done.5.a_ref = bf16[128,1536]{1,0:T(8,128)(2,1)S(1)} collective-permute-done((bf16[128,1536]{1,0:T(8,128)(2,1)S(1)}, bf16[128,1536]{1,0:T(8,128)(2,1)S(1)}, u32[]{:S(2)}, u32[]{:S(2)}) %collective-permute-start.5) | collective-permute-done | bytes 393248 | tf_op jit(solution)/shard_map/ppermute | solution.py:264
  53.4 16.3 %collective-permute-done.6.b_ref = bf16[128,1536]{1,0:T(8,128)(2,1)S(1)} collective-permute-done((bf16[128,1536]{1,0:T(8,128)(2,1)S(1)}, bf16[128,1536]{1,0:T(8,128)(2,1)S(1)}, u32[]{:S(2)}, u32[]{:S(2)}) %collective-permute-start.6) | collective-permute-done | bytes 393248 | tf_op jit(solution)/shard_map/ppermute | solution.py:264
  69.7 0.0 copy-done.6
  69.7 3.1 %early_projection.3.early_ref = bf16[256,3072]{1,0:T(8,128)(2,1)S(1)} custom-call(bf16[128,1536]{1,0:T(8,128)(2,1)S(1)} %collective-permute-done.5.a_ref, bf16[128,1536]{1,0:T(8,128)(2,1)S(1)} %collective-permute-done.6.b_ref, f32[3,1,1536]{2,1,0:T(1,128)S(1)} %bitcast.20, bf16[1536,4608]{1,0:T(8,128)(2,1)S(1)} %bitcast.9), custom_call_target="tpu_custom_call" | custom-call | tf_op jit(solution)/shard_map/early_projection/pallas_call | solution.py:128
  72.8 0.0 collective-permute-done.4.x_ref
  72.9 4.3 %own_projection.3.qkv_ref = bf16[256,4608]{1,0:T(8,128)(2,1)S(1)} custom-call(bf16[256,1536]{1,0:T(8,128)(2,1)S(1)} %collective-permute-done.4.x_ref, f32[3,1,1536]{2,1,0:T(1,128)S(1)} %bitcast.21, bf16[1536,4608]{1,0:T(8,128)(2,1)S(1)} %bitcast.10), custom_call_target="tpu_custom_call" | custom-call | tf_op jit(solution)/shard_map/own_projection/pallas_call | solution.py:109
  77.2 0.0 collective-permute-done.7.c_ref
  77.2 0.0 collective-permute-done.8.d_ref
  77.2 13.2 %tail.3 = bf16[256,1536]{1,0:T(8,128)(2,1)} custom-call(s32[4,16]{1,0:T(4,128)S(1)} %bitcast.25, s32[16]{0:T(128)S(1)} %copy-done.8, bf16[256,1536]{1,0:T(8,128)(2,1)S(1)} %collective-permute-done.4.x_ref, bf16[256,4608]{1,0:T(8,128)(2,1)S(1)} %own_projection.3.qkv_ref, bf16[256,3072]{1,0:T(8,128)(2,1)S(1)} %early_projection.3.early_ref, ...), custom_call_target="tpu_custom_call" | custom-call | tf_op jit(solution)/shard_map/tail/pallas_call | solution.py:225
Async XLA Ops:
  2.4 19.8 %collective-permute-start = (bf16[128,1536]{1,0:T(8,128)(2,1)}, bf16[128,1536]{1,0:T(8,128)(2,1)S(1)}, u32[]{:S(2)}, u32[]{:S(2)}) collective-permute-start(bf16[128,1536]{1,0:T(8,128)(2,1)} %get-tuple-element.14), channel_id=1, source_target_pairs={{0,0},{1,2},{2,1},{3,4},{4,3},{5,6},{6,5},{7,7},{8,8},{9,10},{10,9... | collective-permute-start | bytes 1179656 | tf_op jit(solution)/shard_map/ppermute | solution.py:249
  5.7 19.0 %collective-permute-start.1 = (bf16[128,1536]{1,0:T(8,128)(2,1)}, bf16[128,1536]{1,0:T(8,128)(2,1)S(1)}, u32[]{:S(2)}, u32[]{:S(2)}) collective-permute-start(bf16[128,1536]{1,0:T(8,128)(2,1)} %get-tuple-element.15), channel_id=1, source_target_pairs={{0,1},{1,0},{2,3},{3,2},{4,5},{5,4},{6,7},{7,6},{8,9},{9,8},{10,11... | collective-permute-start | bytes 1179656 | tf_op jit(solution)/shard_map/ppermute | solution.py:249
  7.4 20.4 %collective-permute-start.2 = (bf16[128,1536]{1,0:T(8,128)(2,1)}, bf16[128,1536]{1,0:T(8,128)(2,1)S(1)}, u32[]{:S(2)}, u32[]{:S(2)}) collective-permute-start(bf16[128,1536]{1,0:T(8,128)(2,1)} %get-tuple-element.16), channel_id=1, source_target_pairs={{0,2},{1,3},{2,0},{3,1},{4,6},{5,7},{6,4},{7,5},{8,10},{9,11},{10,... | collective-permute-start | bytes 1179656 | tf_op jit(solution)/shard_map/ppermute | solution.py:249
  7.9 19.9 %collective-permute-start.3 = (bf16[128,1536]{1,0:T(8,128)(2,1)}, bf16[128,1536]{1,0:T(8,128)(2,1)S(1)}, u32[]{:S(2)}, u32[]{:S(2)}) collective-permute-start(bf16[128,1536]{1,0:T(8,128)(2,1)} %get-tuple-element.17), channel_id=1, source_target_pairs={{0,0},{1,1},{2,4},{3,5},{4,2},{5,3},{6,6},{7,7},{8,8},{9,9},{10,12... | collective-permute-start | bytes 1179656 | tf_op jit(solution)/shard_map/ppermute | solution.py:249
  10.9 5.0 %copy-start = (bf16[1,1536,4608]{2,1,0:T(8,128)(2,1)S(1)}, bf16[1,1536,4608]{2,1,0:T(8,128)(2,1)}, u32[]{:S(2)}) copy-start(bf16[1,1536,4608]{2,1,0:T(8,128)(2,1)} %param.7) | copy-start | bytes 42467332
  15.9 1.1 %copy-start.3 = (bf16[1,256,1536]{2,1,0:T(8,128)(2,1)S(1)}, bf16[1,256,1536]{2,1,0:T(8,128)(2,1)}, u32[]{:S(2)}) copy-start(bf16[1,256,1536]{2,1,0:T(8,128)(2,1)} %param.6) | copy-start | bytes 2359300
  17.1 0.7 copy-start.5
  17.8 6.9 %copy-start.1 = (bf16[1,1536,4608]{2,1,0:T(8,128)(2,1)S(1)}, bf16[1,1536,4608]{2,1,0:T(8,128)(2,1)}, u32[]{:S(2)}) copy-start(bf16[1,1536,4608]{2,1,0:T(8,128)(2,1)} %param.7) | copy-start | bytes 42467332
  22.2 5.7 %copy-start.4 = (bf16[1,256,1536]{2,1,0:T(8,128)(2,1)S(1)}, bf16[1,256,1536]{2,1,0:T(8,128)(2,1)}, u32[]{:S(2)}) copy-start(bf16[1,256,1536]{2,1,0:T(8,128)(2,1)} %param.6) | copy-start | bytes 2359300
  22.2 5.7 %copy-start.7 = (s32[16,4]{0,1:T(4,128)S(1)}, s32[16,4]{0,1:T(4,128)}, u32[]{:S(2)}) copy-start(s32[16,4]{0,1:T(4,128)} %param.10) | copy-start | bytes 772
  22.2 5.6 %copy-start.8 = (s32[16]{0:T(128)S(1)}, s32[16]{0:T(128)}, u32[]{:S(2)}) copy-start(s32[16]{0:T(128)} %count_ref.3) | copy-start | bytes 196
  24.7 3.2 %copy-start.2 = (bf16[1,1536,1536]{2,1,0:T(8,128)(2,1)S(1)}, bf16[1,1536,1536]{2,1,0:T(8,128)(2,1)}, u32[]{:S(2)}) copy-start(bf16[1,1536,1536]{2,1,0:T(8,128)(2,1)} %param.8) | copy-start | bytes 14155780
  27.8 41.9 %copy-start.6 = (f32[1,3,1536]{2,0,1:T(1,128)S(1)}, f32[1,3,1536]{2,0,1:T(1,128)}, u32[]{:S(2)}) copy-start(f32[1,3,1536]{2,0,1:T(1,128)} %param.9) | copy-start | bytes 55300
  40.5 32.4 %collective-permute-start.4 = (bf16[256,1536]{1,0:T(8,128)(2,1)S(1)}, bf16[256,1536]{1,0:T(8,128)(2,1)S(1)}, u32[]{:S(2)}, u32[]{:S(2)}) collective-permute-start(bf16[256,1536]{1,0:T(8,128)(2,1)S(1)} %get-tuple-element.18), channel_id=1, source_target_pairs={{0,8},{8,16},{16,24},{24,0},{1,9},{9,17},{17,25},{25,1},{2,10},{10... | collective-permute-start | bytes 2359304 | tf_op jit(solution)/shard_map/ppermute | solution.py:256
  40.5 12.9 %collective-permute-start.5 = (bf16[128,1536]{1,0:T(8,128)(2,1)S(1)}, bf16[128,1536]{1,0:T(8,128)(2,1)S(1)}, u32[]{:S(2)}, u32[]{:S(2)}) collective-permute-start(bf16[128,1536]{1,0:T(8,128)(2,1)S(1)} %get-tuple-element.19), channel_id=1, source_target_pairs={{0,8},{1,10},{2,9},{3,12},{4,11},{5,14},{6,13},{7,15},{8,16},{9,18... | collective-permute-start | bytes 1179656 | tf_op jit(solution)/shard_map/ppermute | solution.py:264
  43.1 26.6 %collective-permute-start.6 = (bf16[128,1536]{1,0:T(8,128)(2,1)S(1)}, bf16[128,1536]{1,0:T(8,128)(2,1)S(1)}, u32[]{:S(2)}, u32[]{:S(2)}) collective-permute-start(bf16[128,1536]{1,0:T(8,128)(2,1)S(1)} %get-tuple-element.20), channel_id=1, source_target_pairs={{0,9},{1,8},{2,11},{3,10},{4,13},{5,12},{6,15},{7,14},{8,17},{9,16... | collective-permute-start | bytes 1179656 | tf_op jit(solution)/shard_map/ppermute | solution.py:264
  44.3 32.9 %collective-permute-start.7 = (bf16[128,1536]{1,0:T(8,128)(2,1)S(1)}, bf16[128,1536]{1,0:T(8,128)(2,1)S(1)}, u32[]{:S(2)}, u32[]{:S(2)}) collective-permute-start(bf16[128,1536]{1,0:T(8,128)(2,1)S(1)} %get-tuple-element.21), channel_id=1, source_target_pairs={{0,10},{1,11},{2,8},{3,9},{4,14},{5,15},{6,12},{7,13},{8,18},{9,19... | collective-permute-start | bytes 1179656 | tf_op jit(solution)/shard_map/ppermute | solution.py:264
  44.9 32.3 %collective-permute-start.8 = (bf16[128,1536]{1,0:T(8,128)(2,1)S(1)}, bf16[128,1536]{1,0:T(8,128)(2,1)S(1)}, u32[]{:S(2)}, u32[]{:S(2)}) collective-permute-start(bf16[128,1536]{1,0:T(8,128)(2,1)S(1)} %get-tuple-element.22), channel_id=1, source_target_pairs={{0,8},{1,9},{2,12},{3,13},{4,10},{5,11},{6,14},{7,15},{8,16},{9,17... | collective-permute-start | bytes 1179656 | tf_op jit(solution)/shard_map/ppermute | solution.py:264

commit v2 on v1

v2 whole, which is shorter than its diff:
```python
import functools

import jax
import jax.numpy as jnp
from jax import lax
from jax.experimental import pallas as pl
from jax.experimental.pallas import tpu as pltpu
from jax.sharding import PartitionSpec as P

HEADS = 12
HD = 128
BLK = 128
EPSILON = 1e-06
INNER = HEADS * HD
PAIR = 2 * HD
TO_EXP2 = HD ** (-0.5) * 1.4426950408889634
MASKED = -1e30
EARLY = (1, 0, 2, 3)
LATE = ()
FIRST_TAKEN = (1,)
LIMIT = 16 * 2**20
FIRST_LIMIT = 30 * 2**20

IN_VMEM = pl.BlockSpec(memory_space=pltpu.VMEM)
IN_SMEM = pl.BlockSpec(memory_space=pltpu.SMEM)
IN_HBM = pl.BlockSpec(memory_space=pltpu.HBM)


def beyond(me, count):
    one = me + 1 - 2 * (me % 2)
    other_one = me - 1 + 2 * (me % 2)
    two = me + 2 - 4 * ((me // 2) % 2)
    other_two = me - 2 + 4 * ((me // 2) % 2)
    return [one, other_one, two, other_two]


def partner_table(count):
    table = []
    for me in range(count):
        table.append([p if 0 <= p < count else me for p in beyond(me, count)])
    return table


def pairs_of(exchange, count):
    table = partner_table(count)
    return [(me, table[me][exchange]) for me in range(count)]


def asked_block(key_ref, target, me, blocks_here):
    width = key_ref.shape[0]
    found = jnp.int32(0)
    for row in range(blocks_here):
        for entry in range(width):
            named = key_ref[entry, target * blocks_here + row]
            mine = (named >= me * blocks_here) & (named < (me + 1) * blocks_here)
            found = jnp.where(mine, named - me * blocks_here, found)
    return found


def partners_here(me, count):
    out = []
    for p in beyond(me, count):
        out.append(jnp.where((p >= 0) & (p < count), p, me))
    return out


def pick_first_kernel(count, exchanges, key_ref, x_in, mod_in, x_ref, mod_ref, *sends):
    send_asked(count, exchanges, key_ref, x_in, sends)
    x_ref[...] = x_in[...]
    mod_ref[...] = mod_in[...]


def pick_first(x, mod, key_blocks, count, exchanges):
    part = jax.ShapeDtypeStruct((BLK, x.shape[1]), x.dtype)
    return pl.pallas_call(
        functools.partial(pick_first_kernel, count, exchanges),
        out_shape=[jax.ShapeDtypeStruct(a.shape, a.dtype) for a in (x, mod)] + [part] * len(exchanges),
        in_specs=[IN_SMEM, IN_VMEM, IN_VMEM],
        out_specs=[IN_VMEM] * (2 + len(exchanges)),
        compiler_params=pltpu.CompilerParams(vmem_limit_bytes=LIMIT),
        name="pick_first",
    )(key_blocks, x, mod)


def pick_kernel(count, exchanges, key_ref, x_ref, *sends):
    send_asked(count, exchanges, key_ref, x_ref, sends)


def pick_blocks(x, key_blocks, count, exchanges):
    part = jax.ShapeDtypeStruct((BLK, x.shape[1]), x.dtype)
    return pl.pallas_call(
        functools.partial(pick_kernel, count, exchanges),
        out_shape=[part] * len(exchanges),
        in_specs=[IN_SMEM, IN_VMEM],
        out_specs=[IN_VMEM] * len(exchanges),
        compiler_params=pltpu.CompilerParams(vmem_limit_bytes=LIMIT),
        name="pick_blocks",
    )(key_blocks, x)


def send_asked(count, exchanges, key_ref, y_ref, sends):
    me = lax.axis_index("seq")
    blocks_here = y_ref.shape[0] // BLK
    for exchange, send in zip(exchanges, sends):
        target = partners_here(me, count)[exchange]
        start = pl.multiple_of(asked_block(key_ref, target, me, blocks_here) * BLK, BLK)
        send[...] = y_ref[pl.ds(start, BLK), :]


def norm_rows(x_ref, mod_ref, out_ref, out_row):
    rows, width = x_ref.shape
    shift = mod_ref[0]
    scale = 1.0 + mod_ref[1]
    step = 16
    for r in range(0, rows, step):
        values = x_ref[r : r + step, :].astype(jnp.float32)
        center = jnp.sum(values, axis=-1, keepdims=True) * (1.0 / width)
        values = values - center
        spread = jnp.sum(values * values, axis=-1, keepdims=True) * (1.0 / width)
        normed = values * lax.rsqrt(spread + EPSILON)
        out_ref[out_row + r : out_row + r + step, :] = (normed * scale + shift).astype(jnp.bfloat16)


def project(source, weight_ref, column, width):
    return jnp.dot(
        source, weight_ref[:, column : column + width], preferred_element_type=jnp.float32
    ).astype(jnp.bfloat16)


def scores_of(q, k):
    return lax.dot_general(q, k, (((1,), (1,)), ((), ())), preferred_element_type=jnp.float32)


def with_ones(v):
    return jnp.concatenate([v, jnp.ones(v.shape, v.dtype)], axis=1)


def own_heads(normed, w_ref, q_ref, kv, peak_ref, total_ref, acc_ref, before):
    wide = 4 * HD
    for n, at in enumerate(range(0, INNER, wide)):
        cols = slice(at, at + wide)
        before(3 * n)
        q_ref[:, cols] = project(normed[...], w_ref, at, wide)
        before(3 * n + 1)
        kv[:, cols] = project(normed[...], w_ref, INNER + at, wide)
        before(3 * n + 2)
        kv[:, INNER + at : INNER + at + wide] = project(normed[...], w_ref, 2 * INNER + at, wide)
        for h in range(at, at + wide, HD):
            here = slice(h, h + HD)
            s = scores_of(q_ref[:, here], kv[:, here])
            peak = jnp.max(s, axis=-1, keepdims=True)
            p = jnp.exp2((s - peak) * TO_EXP2).astype(jnp.bfloat16)
            both = jnp.dot(p, with_ones(kv[:, INNER + h : INNER + h + HD]), preferred_element_type=jnp.float32)
            peak_ref[:, here] = jnp.broadcast_to(peak, (s.shape[0], HD))
            total_ref[:, here] = both[:, HD:]
            acc_ref[:, here] = both[:, :HD]


def first_kernel(
    count, key_ref, x_ref, mod_ref, w_hbm, q_ref, peak_ref, total_ref, acc_ref, w_ref, *rest
):
    sends, (normed, kv, sems) = rest[:-3], rest[-3:]
    wide = 4 * HD
    copies = []
    for at in range(0, INNER, wide):
        for c in (at, INNER + at, 2 * INNER + at):
            n = len(copies)
            cols = slice(c, c + wide)
            copies.append(pltpu.make_async_copy(w_hbm.at[:, cols], w_ref.at[:, cols], sems.at[n]))
            copies[n].start()
    send_asked(count, LATE, key_ref, x_ref, sends)
    norm_rows(x_ref, mod_ref, normed, 0)
    own_heads(normed, w_ref, q_ref, kv, peak_ref, total_ref, acc_ref, lambda n: copies[n].wait())


def own_scratch(tokens, width):
    return [pltpu.VMEM((tokens, width), jnp.bfloat16), pltpu.VMEM((tokens, 2 * INNER), jnp.bfloat16)]


def first_part(x, mod, w, key_blocks, count):
    tokens, width = x.shape
    state = jax.ShapeDtypeStruct((tokens, INNER), jnp.float32)
    held = [jax.ShapeDtypeStruct(shape, jnp.bfloat16) for shape in [(tokens, INNER), w.shape] + [(BLK, width)] * len(LATE)]
    return pl.pallas_call(
        functools.partial(first_kernel, count),
        out_shape=held[:1] + [state] * 3 + held[1:],
        in_specs=[IN_SMEM, IN_VMEM, IN_VMEM, IN_HBM],
        out_specs=[IN_VMEM] * (5 + len(LATE)),
        scratch_shapes=own_scratch(tokens, width) + [pltpu.SemaphoreType.DMA((w.shape[1] // (2 * PAIR),))],
        compiler_params=pltpu.CompilerParams(vmem_limit_bytes=FIRST_LIMIT),
        name="first_part",
    )(key_blocks, x, mod, w)


def second_kernel(count, key_ref, x_ref, mod_ref, w_ref, q_ref, peak_ref, total_ref, acc_ref, *rest):
    sends, (normed, kv) = rest[:-2], rest[-2:]
    send_asked(count, LATE, key_ref, x_ref, sends)
    norm_rows(x_ref, mod_ref, normed, 0)
    own_heads(normed, w_ref, q_ref, kv, peak_ref, total_ref, acc_ref, lambda n: None)


def second_part(x, mod, w, key_blocks, count):
    tokens, width = x.shape
    state = jax.ShapeDtypeStruct((tokens, INNER), jnp.float32)
    return pl.pallas_call(
        functools.partial(second_kernel, count),
        out_shape=[jax.ShapeDtypeStruct((tokens, INNER), jnp.bfloat16)]
        + [state] * 3
        + [jax.ShapeDtypeStruct((BLK, width), x.dtype)] * len(LATE),
        in_specs=[IN_SMEM] + [IN_VMEM] * 3,
        out_specs=[IN_VMEM] * (4 + len(LATE)),
        scratch_shapes=own_scratch(tokens, width),
        compiler_params=pltpu.CompilerParams(vmem_limit_bytes=LIMIT),
        name="second_part",
    )(key_blocks, x, mod, w)


def uses(key_ref, count_ref, me, owner, blocks_here):
    used = jnp.bool_(False)
    for i in range(blocks_here):
        row = me * blocks_here + i
        for j in range(blocks_here, key_ref.shape[0]):
            used = used | ((key_ref[j, row] // blocks_here == owner) & (j < count_ref[row]))
    return used & (owner != me)


def project_block(block_ref, mod_ref, w_ref, normed, row, kv_ref):
    rows = slice(row, row + BLK)
    norm_rows(block_ref, mod_ref, normed, row)
    for c in range(0, 2 * INNER, 2 * PAIR):
        kv_ref[rows, c : c + 2 * PAIR] = project(normed[rows, :], w_ref, INNER + c, 2 * PAIR)


def arrived_kernel(count, exchanges, blocks_here, key_ref, count_ref, *rest):
    blocks, (mod_ref, w_ref, kv_ref, normed) = rest[: len(exchanges)], rest[len(exchanges) :]
    me = lax.axis_index("seq")
    partners = partners_here(me, count)
    for n, exchange in enumerate(exchanges):

        @pl.when(uses(key_ref, count_ref, me, partners[exchange], blocks_here))
        def _():
            project_block(blocks[n], mod_ref, w_ref, normed, n * BLK, kv_ref)


def arrived_part(count, exchanges, blocks_here, key_blocks, block_counts, blocks, mod, w):
    rows = len(exchanges) * BLK
    return pl.pallas_call(
        functools.partial(arrived_kernel, count, exchanges, blocks_here),
        out_shape=jax.ShapeDtypeStruct((rows, 2 * INNER), jnp.bfloat16),
        in_specs=[IN_SMEM] * 2 + [IN_VMEM] * (len(blocks) + 2),
        out_specs=IN_VMEM,
        scratch_shapes=[pltpu.VMEM((rows, w.shape[0]), jnp.bfloat16)],
        compiler_params=pltpu.CompilerParams(vmem_limit_bytes=LIMIT),
        name="arrived_part",
    )(key_blocks, block_counts, *blocks, mod, w)


def last_kernel(
    count, key_ref, count_ref, two_ref, other_one_ref, block_ref, q_ref, peak_ref, total_ref, acc_ref, x_ref, mod_ref,
    w_ref, wo_ref, y_ref, normed, one_ref, attended,
):
    me = lax.axis_index("seq")
    blocks_here = x_ref.shape[0] // BLK
    remote = key_ref.shape[0] - blocks_here
    partners = partners_here(me, count)

    @pl.when(uses(key_ref, count_ref, me, partners[0], blocks_here))
    def _():
        project_block(block_ref, mod_ref, w_ref, normed, 0, one_ref)

    chosen, bias = [], []
    for i in range(blocks_here):
        row = me * blocks_here + i
        owners = [key_ref[blocks_here + j, row] // blocks_here for j in range(remote)]
        live = [blocks_here + j < count_ref[row] for j in range(remote)]
        owners = [jnp.where(live[j], owners[j], owners[0]) for j in range(remote)]
        bias.append([jnp.where(live[j], 0.0, MASKED) for j in range(remote)])
        chosen.append(
            [
                (
                    pl.multiple_of(jnp.where(owner == partners[3], BLK, 0), BLK),
                    owner == partners[1],
                    owner == partners[0],
                )
                for owner in owners
            ]
        )

    def block_of(i, cols):
        parts = []
        for start, is_other_one, is_one in chosen[i]:
            part = two_ref[pl.ds(start, BLK), cols]
            part = jnp.where(is_other_one, other_one_ref[:, cols], part)
            parts.append(jnp.where(is_one, one_ref[:, cols], part))
        return jnp.concatenate(parts, axis=0)

    for at in range(0, INNER, HD):
        here = slice(at, at + HD)
        for i in range(blocks_here):
            rows = slice(i * BLK, (i + 1) * BLK)
            s = scores_of(q_ref[rows, here], block_of(i, here))
            s = [s[:, j * BLK : (j + 1) * BLK] + bias[i][j] for j in range(remote)]
            old_peak = peak_ref[rows, here]
            peak = old_peak
            for part in s:
                peak = jnp.maximum(peak, jnp.max(part, axis=-1, keepdims=True))
            p = jnp.concatenate([jnp.exp2((part - peak) * TO_EXP2).astype(jnp.bfloat16) for part in s], axis=1)
            v = with_ones(block_of(i, slice(INNER + at, INNER + at + HD)))
            both = jnp.dot(p, v, preferred_element_type=jnp.float32)
            keep = jnp.exp2((old_peak - peak) * TO_EXP2)
            total = total_ref[rows, here] * keep + both[:, HD:]
            acc = acc_ref[rows, here] * keep + both[:, :HD]
            attended[rows, here] = (acc / total).astype(jnp.bfloat16)
    for c in range(0, wo_ref.shape[1], 2 * PAIR):
        cols = slice(c, c + 2 * PAIR)
        out = jnp.dot(attended[...], wo_ref[:, cols], preferred_element_type=jnp.float32)
        y_ref[:, cols] = (x_ref[:, cols].astype(jnp.float32) + mod_ref[2, :, cols] * out).astype(jnp.bfloat16)


def last_part(count, key_blocks, block_counts, two, other_one, block, q, state, x, mod, w, wo):
    return pl.pallas_call(
        functools.partial(last_kernel, count),
        out_shape=jax.ShapeDtypeStruct(x.shape, x.dtype),
        in_specs=[IN_SMEM] * 2 + [IN_VMEM] * 11,
        out_specs=IN_VMEM,
        scratch_shapes=[
            pltpu.VMEM((BLK, w.shape[0]), jnp.bfloat16),
            pltpu.VMEM((BLK, 2 * INNER), jnp.bfloat16),
            pltpu.VMEM((x.shape[0], INNER), jnp.bfloat16),
        ],
        compiler_params=pltpu.CompilerParams(vmem_limit_bytes=LIMIT),
        name="last_part",
    )(key_blocks, block_counts, two, other_one, block, q, *state, x, mod, w, wo)


def rest_of_layer(x, q, state, got, mod, w, wo, key_blocks, block_counts, count):
    lists_of = (key_blocks, block_counts)
    blocks_here = x.shape[0] // BLK
    other_one = arrived_part(count, (1,), blocks_here, *lists_of, [got[1]], mod, w)
    two = arrived_part(count, (2, 3), blocks_here, *lists_of, [got[2], got[3]], mod, w)
    return last_part(count, *lists_of, two, other_one, got[0], q, state, x, mod, w, wo)


def exchanged(sends, exchanges, count):
    return {i: lax.ppermute(send, "seq", pairs_of(i, count)) for i, send in zip(exchanges, sends)}


def on_device(activations, qkv_weight, out_weight, modulation, key_blocks, block_counts):
    count = lax.axis_size("seq")
    sections = lax.axis_size("section")
    x, w, wo = activations[0], qkv_weight[0], out_weight[0]
    mod = modulation.reshape(modulation.shape[1], 1, modulation.shape[2])
    key_blocks = key_blocks.T

    x, mod, *sends = pick_first(x, mod, key_blocks, count, EARLY)
    got = exchanged(sends, EARLY, count)
    q, peak, total, acc, w, *sends = first_part(x, mod, w, key_blocks, count)
    got.update(exchanged(sends, LATE, count))
    y = rest_of_layer(x, q, (peak, total, acc), got, mod, w, wo, key_blocks, block_counts, count)

    x = lax.ppermute(y, "section", [(s, (s + 1) % sections) for s in range(sections)])
    sends = pick_blocks(x, key_blocks, count, EARLY)
    got = exchanged(sends, EARLY, count)
    q, peak, total, acc, *sends = second_part(x, mod, w, key_blocks, count)
    got.update(exchanged(sends, LATE, count))
    out = rest_of_layer(x, q, (peak, total, acc), got, mod, w, wo, key_blocks, block_counts, count)
    return out[None]


def solution(mesh):
    return jax.shard_map(
        on_device,
        mesh=mesh,
        in_specs=(
            P("section", "seq", None),
            P("section", None, None),
            P("section", None, None),
            P("section", None, None),
            P(),
            P(),
        ),
        out_specs=P("section", "seq", None),
        check_vma=False,
    )
```

time: 90.8 us -> 77.8 us (0.86)
  the two profiles are of different devices: /device:TPU:8 before, /device:TPU:0 now
where the time goes in v2:
time: 77.8 us; the launch traced here: 77 us
  Pallas kernels  35.9 us (46%)
  waiting for transfers between devices  21.5 us (28%)
  starting transfers between devices  16.2 us (21%)
  local copies, waits for them, and re-layouts  3.24 us (4%)
    ppermute x8, starting transfers between devices, exchanged(): lax.ppermute(send, 'seq', pairs_of(i, count))  16.1 us
    pallas_call x2, Pallas kernels, last_part(): pl.pallas_call(functools.partial(last_kernel, count), out_shape=jax.Shape...  13.5 us
    ppermute x1, waiting for transfers between devices, on_device(): lax.ppermute(y, 'section', [(s, (s + 1) % sections) for s in range(sectio...  11.4 us
    ppermute x8, waiting for transfers between devices, exchanged(): lax.ppermute(send, 'seq', pairs_of(i, count))  10.1 us
    pallas_call x1, Pallas kernels, first_part(): pl.pallas_call(functools.partial(first_kernel, count), out_shape=held[:1]...  8.82 us
    pallas_call x1, Pallas kernels, second_part(): pl.pallas_call(functools.partial(second_kernel, count), out_shape=[jax.Sh...  6.09 us
    pallas_call x4, Pallas kernels, arrived_part(): pl.pallas_call(functools.partial(arrived_kernel, count, exchanges, blocks...  6.06 us
    unnamed x16, local copies, waits for them, and re-layouts  3.24 us
  transfers between devices with their start and end apart: 9, of which 3 were waited for; matrix products, arithmetic and copies ran while one was open for 0% of the time, Pallas kernels for 27%

profile of v2, /device:TPU:0, one launch (start us, length us, event | category | flops | bytes accessed | tf_op | source)
XLA Modules:
  0.0 77.0 jit_solution(14895309964753856634)
XLA Ops:
  0.0 0.0 copy-start
  0.0 1.1 %copy-done = bf16[1,256,1536]{2,1,0:T(8,128)(2,1)S(1)} copy-done((bf16[1,256,1536]{2,1,0:T(8,128)(2,1)S(1)}, bf16[1,256,1536]{2,1,0:T(8,128)(2,1)}, u32[]{:S(2)}) %copy-start) | copy-done | bytes 786456
  1.1 0.0 copy-start.1
  1.1 0.7 copy-done.1
  1.8 0.0 copy-start.4
  1.8 0.7 copy-done.4
  2.5 0.8 pick_first.1
  3.3 0.7 collective-permute-start.2
  4.0 5.7 %collective-permute-start = (bf16[128,1536]{1,0:T(8,128)(2,1)S(1)}, bf16[128,1536]{1,0:T(8,128)(2,1)S(1)}, u32[]{:S(2)}, u32[]{:S(2)}) collective-permute-start(bf16[128,1536]{1,0:T(8,128)(2,1)S(1)} %get-tuple-element.24), channel_id=1, source_target_pairs={{0,2},{1,3},{2,0},{3,1},{4,6},{5,7},{6,4},{7,5},{8,10},{9,11},{10,... | collective-permute-start | bytes 1179656 | tf_op jit(solution)/shard_map/ppermute | solution.py:345
  9.7 0.7 collective-permute-start.1
  10.4 1.7 %collective-permute-start.3 = (bf16[128,1536]{1,0:T(8,128)(2,1)S(1)}, bf16[128,1536]{1,0:T(8,128)(2,1)S(1)}, u32[]{:S(2)}, u32[]{:S(2)}) collective-permute-start(bf16[128,1536]{1,0:T(8,128)(2,1)S(1)} %get-tuple-element.30), channel_id=1, source_target_pairs={{0,1},{1,0},{2,3},{3,2},{4,5},{5,4},{6,7},{7,6},{8,9},{9,8},{10,11... | collective-permute-start | bytes 1179656 | tf_op jit(solution)/shard_map/ppermute | solution.py:345
  12.1 0.0 copy-start.2
  12.1 0.7 copy-done.2
  12.8 0.0 copy-start.5
  12.8 8.8 %first_part.1 = (bf16[256,1536]{1,0:T(8,128)(2,1)S(1)}, f32[256,1536]{1,0:T(8,128)S(1)}, f32[256,1536]{1,0:T(8,128)S(1)}, f32[256,1536]{1,0:T(8,128)S(1)}, bf16[1536,4608]{1,0:T(8,128)(2,1)S(1)}) custom-call(s32[4,16]{1,0:T(4,128)S(1)} %bitcast.12, bf16[256,1536]{1,0:T(8,128)(2,1)S(1)} %get-tuple-element.27.x_ref, ...), custom_call_target="tpu_custom_call" | custom-call | tf_op jit(solution)/shard_map/first_part/pallas_call | solution.py:184
  21.6 0.0 collective-permute-done.2.rest_0_
  21.6 0.0 copy-done.5
  21.6 0.0 slice-start
  21.6 0.6 arrived_part.5.other_one_ref
  22.3 0.0 slice-start.1
  22.3 4.6 %collective-permute-done.rest_0_ = bf16[128,1536]{1,0:T(8,128)(2,1)S(1)} collective-permute-done((bf16[128,1536]{1,0:T(8,128)(2,1)S(1)}, bf16[128,1536]{1,0:T(8,128)(2,1)S(1)}, u32[]{:S(2)}, u32[]{:S(2)}) %collective-permute-start) | collective-permute-done | bytes 393248 | tf_op jit(solution)/shard_map/ppermute | solution.py:345
  26.9 0.0 collective-permute-done.1.rest_1_
  26.9 2.3 %arrived_part.4.two_ref = bf16[256,3072]{1,0:T(8,128)(2,1)S(1)} custom-call(s32[4,16]{1,0:T(4,128)S(1)} %bitcast.14, s32[16]{0:T(128)S(1)} %copy-done.5, bf16[128,1536]{1,0:T(8,128)(2,1)S(1)} %collective-permute-done.rest_0_, bf16[128,1536]{1,0:T(8,128)(2,1)S(1)} %collective-permute-done.1.rest_1_, ...), custom_call_target="tpu_custom_call" | custom-call | tf_op jit(solution)/shard_map/arrived_part/pallas_call | solution.py:247
  29.2 0.0 collective-permute-done.3.block_ref
  29.3 0.0 slice-done
  29.3 0.0 slice-done.1
  29.3 0.0 copy-start.3
  29.3 6.4 %last_part.2 = bf16[256,1536]{1,0:T(8,128)(2,1)S(1)} custom-call(s32[4,16]{1,0:T(4,128)S(1)} %bitcast.15, s32[16]{0:T(128)S(1)} %copy-done.5, bf16[256,3072]{1,0:T(8,128)(2,1)S(1)} %arrived_part.4.two_ref, bf16[128,3072]{1,0:T(8,128)(2,1)S(1)} %arrived_part.5.other_one_ref, bf16[128,1536]{1,0:T(8,128)(2,1)S(1)} %collective-permute-done.3.block_ref, ...), custom_call_target="tpu_custom_call" | custom-call | tf_op jit(solution)/shard_map/last_part/pallas_call | solution.py:321
  35.7 0.1 collective-permute-start.4
  35.8 11.4 %collective-permute-done.4.x_ref = bf16[256,1536]{1,0:T(8,128)(2,1)S(1)} collective-permute-done((bf16[256,1536]{1,0:T(8,128)(2,1)S(1)}, bf16[256,1536]{1,0:T(8,128)(2,1)S(1)}, u32[]{:S(2)}, u32[]{:S(2)}) %collective-permute-start.4) | collective-permute-done | bytes 786464 | tf_op jit(solution)/shard_map/ppermute | solution.py:361
  47.2 0.7 pick_blocks.1
  47.9 0.7 collective-permute-start.7
  48.6 2.4 %collective-permute-start.5 = (bf16[128,1536]{1,0:T(8,128)(2,1)S(1)}, bf16[128,1536]{1,0:T(8,128)(2,1)S(1)}, u32[]{:S(2)}, u32[]{:S(2)}) collective-permute-start(bf16[128,1536]{1,0:T(8,128)(2,1)S(1)} %get-tuple-element.35), channel_id=1, source_target_pairs={{0,2},{1,3},{2,0},{3,1},{4,6},{5,7},{6,4},{7,5},{8,10},{9,11},{10,... | collective-permute-start | bytes 1179656 | tf_op jit(solution)/shard_map/ppermute | solution.py:345
  51.0 0.7 collective-permute-start.6
  51.6 3.6 %collective-permute-start.8 = (bf16[128,1536]{1,0:T(8,128)(2,1)S(1)}, bf16[128,1536]{1,0:T(8,128)(2,1)S(1)}, u32[]{:S(2)}, u32[]{:S(2)}) collective-permute-start(bf16[128,1536]{1,0:T(8,128)(2,1)S(1)} %get-tuple-element.38), channel_id=1, source_target_pairs={{0,1},{1,0},{2,3},{3,2},{4,5},{5,4},{6,7},{7,6},{8,9},{9,8},{10,11... | collective-permute-start | bytes 1179656 | tf_op jit(solution)/shard_map/ppermute | solution.py:345
  55.2 0.0 copy-done.3
  55.3 6.1 %second_part.1 = (bf16[256,1536]{1,0:T(8,128)(2,1)S(1)}, f32[256,1536]{1,0:T(8,128)S(1)}, f32[256,1536]{1,0:T(8,128)S(1)}, f32[256,1536]{1,0:T(8,128)S(1)}) custom-call(s32[4,16]{1,0:T(4,128)S(1)} %bitcast.17, bf16[256,1536]{1,0:T(8,128)(2,1)S(1)} %collective-permute-done.4.x_ref, f32[3,1,1536]{2,1,0:T(1,128)S(1)} %get-tuple-element.26.mod_ref.rest_2_.rest_1_, ...), custom_call_target="tpu_custom_call" | custom-call | tf_op jit(solution)/shard_map/second_part/pallas_call | solution.py:205
  61.3 0.0 collective-permute-done.7.rest_0_
  61.4 0.6 arrived_part.7.other_one_ref
  62.0 5.5 %collective-permute-done.5.rest_0_ = bf16[128,1536]{1,0:T(8,128)(2,1)S(1)} collective-permute-done((bf16[128,1536]{1,0:T(8,128)(2,1)S(1)}, bf16[128,1536]{1,0:T(8,128)(2,1)S(1)}, u32[]{:S(2)}, u32[]{:S(2)}) %collective-permute-start.5) | collective-permute-done | bytes 393248 | tf_op jit(solution)/shard_map/ppermute | solution.py:345
  67.5 0.0 collective-permute-done.6.rest_1_
  67.5 2.5 %arrived_part.6.two_ref = bf16[256,3072]{1,0:T(8,128)(2,1)S(1)} custom-call(s32[4,16]{1,0:T(4,128)S(1)} %bitcast.19, s32[16]{0:T(128)S(1)} %copy-done.5, bf16[128,1536]{1,0:T(8,128)(2,1)S(1)} %collective-permute-done.5.rest_0_, bf16[128,1536]{1,0:T(8,128)(2,1)S(1)} %collective-permute-done.6.rest_1_, ...), custom_call_target="tpu_custom_call" | custom-call | tf_op jit(solution)/shard_map/arrived_part/pallas_call | solution.py:247
  70.0 0.0 collective-permute-done.8.block_ref
  70.0 7.0 %last_part.3 = bf16[256,1536]{1,0:T(8,128)(2,1)} custom-call(s32[4,16]{1,0:T(4,128)S(1)} %bitcast.20, s32[16]{0:T(128)S(1)} %copy-done.5, bf16[256,3072]{1,0:T(8,128)(2,1)S(1)} %arrived_part.6.two_ref, bf16[128,3072]{1,0:T(8,128)(2,1)S(1)} %arrived_part.7.other_one_ref, bf16[128,1536]{1,0:T(8,128)(2,1)S(1)} %collective-permute-done.8.block_ref, ...), custom_call_target="tpu_custom_call" | custom-call | tf_op jit(solution)/shard_map/last_part/pallas_call | solution.py:321
  (1 shorter events, 0.0 us)
Async XLA Ops:
  0.0 1.1 %copy-start = (bf16[1,256,1536]{2,1,0:T(8,128)(2,1)S(1)}, bf16[1,256,1536]{2,1,0:T(8,128)(2,1)}, u32[]{:S(2)}) copy-start(bf16[1,256,1536]{2,1,0:T(8,128)(2,1)} %param.6) | copy-start | bytes 2359300
  1.1 0.7 copy-start.1
  1.8 0.7 copy-start.4
  3.3 18.3 %collective-permute-start.2 = (bf16[128,1536]{1,0:T(8,128)(2,1)S(1)}, bf16[128,1536]{1,0:T(8,128)(2,1)S(1)}, u32[]{:S(2)}, u32[]{:S(2)}) collective-permute-start(bf16[128,1536]{1,0:T(8,128)(2,1)S(1)} %get-tuple-element.29), channel_id=1, source_target_pairs={{0,0},{1,2},{2,1},{3,4},{4,3},{5,6},{6,5},{7,7},{8,8},{9,10},{10,9... | collective-permute-start | bytes 1179656 | tf_op jit(solution)/shard_map/ppermute | solution.py:345
  4.0 22.9 %collective-permute-start = (bf16[128,1536]{1,0:T(8,128)(2,1)S(1)}, bf16[128,1536]{1,0:T(8,128)(2,1)S(1)}, u32[]{:S(2)}, u32[]{:S(2)}) collective-permute-start(bf16[128,1536]{1,0:T(8,128)(2,1)S(1)} %get-tuple-element.24), channel_id=1, source_target_pairs={{0,2},{1,3},{2,0},{3,1},{4,6},{5,7},{6,4},{7,5},{8,10},{9,11},{10,... | collective-permute-start | bytes 1179656 | tf_op jit(solution)/shard_map/ppermute | solution.py:345
  9.7 17.2 %collective-permute-start.1 = (bf16[128,1536]{1,0:T(8,128)(2,1)S(1)}, bf16[128,1536]{1,0:T(8,128)(2,1)S(1)}, u32[]{:S(2)}, u32[]{:S(2)}) collective-permute-start(bf16[128,1536]{1,0:T(8,128)(2,1)S(1)} %get-tuple-element.25), channel_id=1, source_target_pairs={{0,0},{1,1},{2,4},{3,5},{4,2},{5,3},{6,6},{7,7},{8,8},{9,9},{10,12... | collective-permute-start | bytes 1179656 | tf_op jit(solution)/shard_map/ppermute | solution.py:345
  10.4 18.8 %collective-permute-start.3 = (bf16[128,1536]{1,0:T(8,128)(2,1)S(1)}, bf16[128,1536]{1,0:T(8,128)(2,1)S(1)}, u32[]{:S(2)}, u32[]{:S(2)}) collective-permute-start(bf16[128,1536]{1,0:T(8,128)(2,1)S(1)} %get-tuple-element.30), channel_id=1, source_target_pairs={{0,1},{1,0},{2,3},{3,2},{4,5},{5,4},{6,7},{7,6},{8,9},{9,8},{10,11... | collective-permute-start | bytes 1179656 | tf_op jit(solution)/shard_map/ppermute | solution.py:345
  12.1 0.7 copy-start.2
  12.8 8.8 %copy-start.5 = (s32[16]{0:T(128)S(1)}, s32[16]{0:T(128)}, u32[]{:S(2)}) copy-start(s32[16]{0:T(128)} %count_ref.11) | copy-start | bytes 196
  21.6 7.6 %slice-start = ((s8[4718592]{0:T(1024)(128)(4,1)}), s8[4194304]{0:T(1024)(128)(4,1)S(1)}, s32[]{:S(2)}) async-start(s8[4718592]{0:T(1024)(128)(4,1)} %bitcast.6), calls=%async_computation | async-start | bytes 8388608
  22.3 7.0 %slice-start.1 = ((s8[4718592]{0:T(1024)(128)(4,1)}), s8[524288]{0:T(1024)(128)(4,1)S(1)}, s32[]{:S(2)}) async-start(s8[4718592]{0:T(1024)(128)(4,1)} %bitcast.6), calls=%async_computation.1 | async-start | bytes 1048576
  29.3 26.0 %copy-start.3 = (s32[16,4]{0,1:T(4,128)S(1)}, s32[16,4]{0,1:T(4,128)}, u32[]{:S(2)}) copy-start(s32[16,4]{0,1:T(4,128)} %param.10) | copy-start | bytes 772
  35.7 11.5 %collective-permute-start.4 = (bf16[256,1536]{1,0:T(8,128)(2,1)S(1)}, bf16[256,1536]{1,0:T(8,128)(2,1)S(1)}, u32[]{:S(2)}, u32[]{:S(2)}) collective-permute-start(bf16[256,1536]{1,0:T(8,128)(2,1)S(1)} %last_part.2), channel_id=1, source_target_pairs={{0,8},{8,16},{16,24},{24,0},{1,9},{9,17},{17,25},{25,1},{2,10},{10... | collective-permute-start | bytes 2359304 | tf_op jit(solution)/shard_map/ppermute | solution.py:361
  47.9 13.4 %collective-permute-start.7 = (bf16[128,1536]{1,0:T(8,128)(2,1)S(1)}, bf16[128,1536]{1,0:T(8,128)(2,1)S(1)}, u32[]{:S(2)}, u32[]{:S(2)}) collective-permute-start(bf16[128,1536]{1,0:T(8,128)(2,1)S(1)} %get-tuple-element.37), channel_id=1, source_target_pairs={{0,0},{1,2},{2,1},{3,4},{4,3},{5,6},{6,5},{7,7},{8,8},{9,10},{10,9... | collective-permute-start | bytes 1179656 | tf_op jit(solution)/shard_map/ppermute | solution.py:345
  48.6 18.9 %collective-permute-start.5 = (bf16[128,1536]{1,0:T(8,128)(2,1)S(1)}, bf16[128,1536]{1,0:T(8,128)(2,1)S(1)}, u32[]{:S(2)}, u32[]{:S(2)}) collective-permute-start(bf16[128,1536]{1,0:T(8,128)(2,1)S(1)} %get-tuple-element.35), channel_id=1, source_target_pairs={{0,2},{1,3},{2,0},{3,1},{4,6},{5,7},{6,4},{7,5},{8,10},{9,11},{10,... | collective-permute-start | bytes 1179656 | tf_op jit(solution)/shard_map/ppermute | solution.py:345
  51.0 16.5 %collective-permute-start.6 = (bf16[128,1536]{1,0:T(8,128)(2,1)S(1)}, bf16[128,1536]{1,0:T(8,128)(2,1)S(1)}, u32[]{:S(2)}, u32[]{:S(2)}) collective-permute-start(bf16[128,1536]{1,0:T(8,128)(2,1)S(1)} %get-tuple-element.36), channel_id=1, source_target_pairs={{0,0},{1,1},{2,4},{3,5},{4,2},{5,3},{6,6},{7,7},{8,8},{9,9},{10,12... | collective-permute-start | bytes 1179656 | tf_op jit(solution)/shard_map/ppermute | solution.py:345
  51.6 18.4 %collective-permute-start.8 = (bf16[128,1536]{1,0:T(8,128)(2,1)S(1)}, bf16[128,1536]{1,0:T(8,128)(2,1)S(1)}, u32[]{:S(2)}, u32[]{:S(2)}) collective-permute-start(bf16[128,1536]{1,0:T(8,128)(2,1)S(1)} %get-tuple-element.38), channel_id=1, source_target_pairs={{0,1},{1,0},{2,3},{3,2},{4,5},{5,4},{6,7},{7,6},{8,9},{9,8},{10,11... | collective-permute-start | bytes 1179656 | tf_op jit(solution)/shard_map/ppermute | solution.py:345

commit v3 on v2

v3 whole, which is shorter than its diff:
```python
import functools

import jax
import jax.numpy as jnp
from jax import lax
from jax.experimental import pallas as pl
from jax.experimental.pallas import tpu as pltpu
from jax.sharding import PartitionSpec as P

HEADS = 12
HD = 128
BLK = 128
EPSILON = 1e-06
INNER = HEADS * HD
PAIR = 2 * HD
TO_EXP2 = HD ** (-0.5) * 1.4426950408889634
MASKED = -1e30
EARLY = 1
LATE = (0, 2, 3)
PIECES = 2
DIRECT = (1,)
LIMIT = 16 * 2**20
FIRST_LIMIT = 30 * 2**20

IN_VMEM = pl.BlockSpec(memory_space=pltpu.VMEM)
IN_SMEM = pl.BlockSpec(memory_space=pltpu.SMEM)
IN_HBM = pl.BlockSpec(memory_space=pltpu.HBM)


def beyond(me, count):
    one = me + 1 - 2 * (me % 2)
    other_one = me - 1 + 2 * (me % 2)
    two = me + 2 - 4 * ((me // 2) % 2)
    other_two = me - 2 + 4 * ((me // 2) % 2)
    return [one, other_one, two, other_two]


def partner_table(count):
    table = []
    for me in range(count):
        table.append([p if 0 <= p < count else me for p in beyond(me, count)])
    return table


def pairs_of(exchange, count):
    table = partner_table(count)
    return [(me, table[me][exchange]) for me in range(count)]


def asked_block(key_ref, target, me, blocks_here):
    width = key_ref.shape[0]
    found = jnp.int32(0)
    for row in range(blocks_here):
        for entry in range(width):
            named = key_ref[entry, target * blocks_here + row]
            mine = (named >= me * blocks_here) & (named < (me + 1) * blocks_here)
            found = jnp.where(mine, named - me * blocks_here, found)
    return found


def partners_here(me, count):
    out = []
    for p in beyond(me, count):
        out.append(jnp.where((p >= 0) & (p < count), p, me))
    return out


def pick_kernel(count, exchanges, parts, key_ref, *refs):
    send_asked(count, exchanges, key_ref, refs[:parts], refs[parts:])


def pick_blocks(parts, key_blocks, count, exchanges, params=None):
    width = parts[0].shape[1]
    return pl.pallas_call(
        functools.partial(pick_kernel, count, exchanges, len(parts)),
        out_shape=[jax.ShapeDtypeStruct((BLK, width), parts[0].dtype)] * len(exchanges),
        in_specs=[IN_SMEM] + [IN_VMEM] * len(parts),
        out_specs=[IN_VMEM] * len(exchanges),
        compiler_params=params,
        name="pick_blocks",
    )(key_blocks, *parts)


def send_asked(count, exchanges, key_ref, parts, sends):
    me = lax.axis_index("seq")
    rows = parts[0].shape[0]
    blocks_here = len(parts) * rows // BLK
    for exchange, send in zip(exchanges, sends):
        block = asked_block(key_ref, partners_here(me, count)[exchange], me, blocks_here)
        if len(parts) == 1:
            send[...] = parts[0][pl.ds(pl.multiple_of(block * BLK, BLK), BLK), :]
        else:
            each = BLK // rows
            for n in range(blocks_here):

                @pl.when(block == n)
                def _():
                    for m in range(each):
                        send[m * rows : (m + 1) * rows, :] = parts[n * each + m][...]


def norm_rows(x_ref, mod_ref, out_ref, out_row):
    rows, width = x_ref.shape
    shift = mod_ref[0]
    scale = 1.0 + mod_ref[1]
    step = 16
    for r in range(0, rows, step):
        values = x_ref[r : r + step, :].astype(jnp.float32)
        center = jnp.sum(values, axis=-1, keepdims=True) * (1.0 / width)
        values = values - center
        spread = jnp.sum(values * values, axis=-1, keepdims=True) * (1.0 / width)
        normed = values * lax.rsqrt(spread + EPSILON)
        out_ref[out_row + r : out_row + r + step, :] = (normed * scale + shift).astype(jnp.bfloat16)


def project(source, weight_ref, column, width):
    return jnp.dot(
        source, weight_ref[:, column : column + width], preferred_element_type=jnp.float32
    ).astype(jnp.bfloat16)


def scores_of(q, k):
    return lax.dot_general(q, k, (((1,), (1,)), ((), ())), preferred_element_type=jnp.float32)


def with_ones(v):
    return jnp.concatenate([v, jnp.ones(v.shape, v.dtype)], axis=1)


def own_columns():
    wide = 4 * HD
    for at in range(0, INNER, wide):
        yield at, wide


def own_heads(normed, w_ref, q_ref, kv, peak_ref, total_ref, acc_ref, row, before):
    rows = slice(row, q_ref.shape[0])
    for n, (at, wide) in enumerate(own_columns()):
        cols = slice(at, at + wide)
        before(3 * n)
        q_ref[rows, cols] = project(normed[...], w_ref, at, wide)
        before(3 * n + 1)
        kv[rows, cols] = project(normed[...], w_ref, INNER + at, wide)
        before(3 * n + 2)
        kv[rows, INNER + at : INNER + at + wide] = project(normed[...], w_ref, 2 * INNER + at, wide)
        for h in range(at, at + wide, HD):
            here = slice(h, h + HD)
            s = scores_of(q_ref[:, here], kv[:, here])
            peak = jnp.max(s, axis=-1, keepdims=True)
            p = jnp.exp2((s - peak) * TO_EXP2).astype(jnp.bfloat16)
            both = jnp.dot(p, with_ones(kv[:, INNER + h : INNER + h + HD]), preferred_element_type=jnp.float32)
            peak_ref[:, here] = jnp.broadcast_to(peak, (s.shape[0], HD))
            total_ref[:, here] = both[:, HD:]
            acc_ref[:, here] = both[:, :HD]


def first_kernel(
    x_ref, mod_ref, w_hbm, q_ref, peak_ref, total_ref, acc_ref, w_ref, normed, kv, sems
):
    wide = 4 * HD
    copies = []
    for at in range(0, INNER, wide):
        for c in (at, INNER + at, 2 * INNER + at):
            n = len(copies)
            cols = slice(c, c + wide)
            copies.append(pltpu.make_async_copy(w_hbm.at[:, cols], w_ref.at[:, cols], sems.at[n]))
            copies[n].start()
    norm_rows(x_ref, mod_ref, normed, 0)
    own_heads(normed, w_ref, q_ref, kv, peak_ref, total_ref, acc_ref, 0, lambda n: copies[n].wait())


def own_scratch(tokens, width):
    return [pltpu.VMEM((tokens, width), jnp.bfloat16), pltpu.VMEM((tokens, 2 * INNER), jnp.bfloat16)]


def first_part(x, mod, w):
    tokens, width = x.shape
    state = jax.ShapeDtypeStruct((tokens, INNER), jnp.float32)
    held = [jax.ShapeDtypeStruct(shape, jnp.bfloat16) for shape in [(tokens, INNER), w.shape]]
    return pl.pallas_call(
        first_kernel,
        out_shape=held[:1] + [state] * 3 + held[1:],
        in_specs=[IN_VMEM, IN_VMEM, IN_HBM],
        out_specs=[IN_VMEM] * 5,
        scratch_shapes=own_scratch(tokens, width) + [pltpu.SemaphoreType.DMA((w.shape[1] // (2 * PAIR),))],
        compiler_params=pltpu.CompilerParams(vmem_limit_bytes=FIRST_LIMIT),
        name="first_part",
    )(x, mod, w)


def half_kernel(x_ref, mod_ref, w_ref, qkv_ref, normed):
    norm_rows(x_ref, mod_ref, normed, 0)
    for c in range(0, 3 * INNER, 4 * HD):
        qkv_ref[:, c : c + 4 * HD] = project(normed[...], w_ref, c, 4 * HD)


def half_part(x, mod, w):
    rows, width = x.shape
    return pl.pallas_call(
        half_kernel,
        out_shape=jax.ShapeDtypeStruct((rows, w.shape[1]), jnp.bfloat16),
        in_specs=[IN_VMEM] * 3,
        out_specs=IN_VMEM,
        scratch_shapes=[pltpu.VMEM((rows, width), jnp.bfloat16)],
        compiler_params=pltpu.CompilerParams(vmem_limit_bytes=LIMIT),
        name="half_part",
    )(x, mod, w)


def second_kernel(a_ref, b_ref, qkv_ref, mod_ref, w_ref, x_ref, q_ref, peak_ref, total_ref, acc_ref, normed, kv):
    rows = a_ref.shape[0]
    x_ref[:rows, :] = a_ref[...]
    x_ref[rows:, :] = b_ref[...]
    q_ref[:rows, :] = qkv_ref[:, :INNER]
    kv[:rows, :] = qkv_ref[:, INNER:]
    norm_rows(b_ref, mod_ref, normed, 0)
    own_heads(normed, w_ref, q_ref, kv, peak_ref, total_ref, acc_ref, rows, lambda n: None)


def second_part(a, b, qkv, mod, w):
    tokens, width = a.shape[0] + b.shape[0], a.shape[1]
    state = jax.ShapeDtypeStruct((tokens, INNER), jnp.float32)
    half = [jax.ShapeDtypeStruct(shape, jnp.bfloat16) for shape in ((tokens, width), (tokens, INNER))]
    return pl.pallas_call(
        second_kernel,
        out_shape=half + [state] * 3,
        in_specs=[IN_VMEM] * 5,
        out_specs=[IN_VMEM] * 5,
        scratch_shapes=[
            pltpu.VMEM(b.shape, jnp.bfloat16),
            pltpu.VMEM((tokens, 2 * INNER), jnp.bfloat16),
        ],
        compiler_params=pltpu.CompilerParams(vmem_limit_bytes=LIMIT),
        name="second_part",
    )(a, b, qkv, mod, w)


def uses(key_ref, count_ref, me, owner, blocks_here):
    used = jnp.bool_(False)
    for i in range(blocks_here):
        row = me * blocks_here + i
        for j in range(blocks_here, key_ref.shape[0]):
            used = used | ((key_ref[j, row] // blocks_here == owner) & (j < count_ref[row]))
    return used & (owner != me)


def project_block(block_ref, mod_ref, w_ref, normed, row, kv_ref):
    rows = slice(row, row + BLK)
    norm_rows(block_ref, mod_ref, normed, row)
    for c in range(0, 2 * INNER, 2 * PAIR):
        kv_ref[rows, c : c + 2 * PAIR] = project(normed[rows, :], w_ref, INNER + c, 2 * PAIR)


def arrived_kernel(count, exchanges, blocks_here, key_ref, count_ref, *rest):
    blocks, (mod_ref, w_ref, kv_ref, normed) = rest[: len(exchanges)], rest[len(exchanges) :]
    me = lax.axis_index("seq")
    partners = partners_here(me, count)
    for n, exchange in enumerate(exchanges):

        @pl.when(uses(key_ref, count_ref, me, partners[exchange], blocks_here))
        def _():
            project_block(blocks[n], mod_ref, w_ref, normed, n * BLK, kv_ref)


def arrived_part(count, exchanges, blocks_here, key_blocks, block_counts, blocks, mod, w):
    rows = len(exchanges) * BLK
    return pl.pallas_call(
        functools.partial(arrived_kernel, count, exchanges, blocks_here),
        out_shape=jax.ShapeDtypeStruct((rows, 2 * INNER), jnp.bfloat16),
        in_specs=[IN_SMEM] * 2 + [IN_VMEM] * (len(blocks) + 2),
        out_specs=IN_VMEM,
        scratch_shapes=[pltpu.VMEM((rows, w.shape[0]), jnp.bfloat16)],
        compiler_params=pltpu.CompilerParams(vmem_limit_bytes=LIMIT),
        name="arrived_part",
    )(key_blocks, block_counts, *blocks, mod, w)


def last_kernel(count, early, late, asked, pieces, key_ref, count_ref, *rest):
    early_refs, rest = rest[: len(early)], rest[len(early) :]
    blocks, rest = rest[: len(late)], rest[len(late) :]
    q_ref, peak_ref, total_ref, acc_ref, x_ref, mod_ref, w_ref, wo_ref, *rest = rest
    ys, sends, (normed, kv, attended) = rest[:pieces], rest[pieces:-3], rest[-3:]
    me = lax.axis_index("seq")
    tokens = x_ref.shape[0]
    blocks_here = tokens // BLK
    remote = key_ref.shape[0] - blocks_here
    partners = partners_here(me, count)
    slots = early + late
    for n, exchange in enumerate(slots):

        @pl.when(uses(key_ref, count_ref, me, partners[exchange], blocks_here))
        def _():
            if n < len(early):
                kv[n * BLK : (n + 1) * BLK, :] = early_refs[n][...]
            else:
                project_block(blocks[n - len(early)], mod_ref, w_ref, normed, n * BLK, kv)

    starts, bias = [], []
    for i in range(blocks_here):
        row = me * blocks_here + i
        starts.append([])
        bias.append([])
        for j in range(remote):
            live = blocks_here + j < count_ref[row]
            bias[i].append(jnp.where(live, 0.0, MASKED))
            owner = key_ref[blocks_here + j, row] // blocks_here
            owner = jnp.where(live, owner, key_ref[blocks_here, row] // blocks_here)
            start = jnp.int32(0)
            for n, exchange in enumerate(slots):
                start = jnp.where(owner == partners[exchange], n * BLK, start)
            starts[i].append(pl.multiple_of(start, BLK))

    def listed(i, cols):
        return jnp.concatenate([kv[pl.ds(start, BLK), cols] for start in starts[i]], axis=0)

    for at in range(0, INNER, HD):
        here = slice(at, at + HD)
        for i in range(blocks_here):
            rows = slice(i * BLK, (i + 1) * BLK)
            s = scores_of(q_ref[rows, here], listed(i, here))
            s = [s[:, j * BLK : (j + 1) * BLK] + bias[i][j] for j in range(remote)]
            old_peak = peak_ref[rows, here]
            peak = old_peak
            for part in s:
                peak = jnp.maximum(peak, jnp.max(part, axis=-1, keepdims=True))
            p = jnp.concatenate([jnp.exp2((part - peak) * TO_EXP2).astype(jnp.bfloat16) for part in s], axis=1)
            v = with_ones(listed(i, slice(INNER + at, INNER + at + HD)))
            both = jnp.dot(p, v, preferred_element_type=jnp.float32)
            keep = jnp.exp2((old_peak - peak) * TO_EXP2)
            total = total_ref[rows, here] * keep + both[:, HD:]
            acc = acc_ref[rows, here] * keep + both[:, :HD]
            attended[rows, here] = (acc / total).astype(jnp.bfloat16)
    for c in range(0, wo_ref.shape[1], 2 * PAIR):
        cols = slice(c, c + 2 * PAIR)
        out = jnp.dot(attended[...], wo_ref[:, cols], preferred_element_type=jnp.float32)
        y = (x_ref[:, cols].astype(jnp.float32) + mod_ref[2, :, cols] * out).astype(jnp.bfloat16)
        for n, y_ref in enumerate(ys):
            rows = tokens // pieces
            y_ref[:, cols] = y[n * rows : (n + 1) * rows]
    send_asked(count, asked, key_ref, ys, sends)


def last_part(count, late, asked, pieces, key_blocks, block_counts, early, blocks, q, state, x, mod, w, wo):
    part = jax.ShapeDtypeStruct((BLK, x.shape[1]), x.dtype)
    piece = jax.ShapeDtypeStruct((x.shape[0] // pieces, x.shape[1]), x.dtype)
    slots = len(early) + len(late)
    return pl.pallas_call(
        functools.partial(last_kernel, count, (EARLY,) * len(early), late, asked, pieces),
        out_shape=[piece] * pieces + [part] * len(asked),
        in_specs=[IN_SMEM] * 2 + [IN_VMEM] * (8 + slots),
        out_specs=[IN_VMEM] * (pieces + len(asked)),
        scratch_shapes=[
            pltpu.VMEM((slots * BLK, w.shape[0]), jnp.bfloat16),
            pltpu.VMEM((slots * BLK, 2 * INNER), jnp.bfloat16),
            pltpu.VMEM((x.shape[0], INNER), jnp.bfloat16),
        ],
        compiler_params=pltpu.CompilerParams(vmem_limit_bytes=LIMIT),
        name="last_part",
    )(key_blocks, block_counts, *early, *blocks, q, *state, x, mod, w, wo)


def on_device(activations, qkv_weight, out_weight, modulation, key_blocks, block_counts):
    count = lax.axis_size("seq")
    sections = lax.axis_size("section")
    x, w, wo = activations[0], qkv_weight[0], out_weight[0]
    mod = modulation.reshape(modulation.shape[1], 1, modulation.shape[2])
    key_blocks = key_blocks.T
    lists_of = (key_blocks, block_counts)
    here = [(s, s) for s in range(sections)]
    onward = [(s, (s + 1) % sections) for s in range(sections)]

    def exchange(send, i, hops):
        pairs = [(s * count + a, t * count + b) for s, t in hops for a, b in pairs_of(i, count)]
        return lax.ppermute(send, ("section", "seq"), pairs)

    order = (EARLY,) + LATE
    got = {i: exchange(send, i, here) for i, send in zip(order, pick_blocks([x], key_blocks, count, order))}
    q, *state, w = first_part(x, mod, w)
    early = [arrived_part(count, (EARLY,), x.shape[0] // BLK, *lists_of, [got[EARLY]], mod, w)]
    blocks = [got[i] for i in LATE]
    made = last_part(count, LATE, DIRECT, PIECES, *lists_of, early, blocks, q, state, x, mod, w, wo)
    pieces, sends = made[:PIECES], made[PIECES:]

    pieces = [lax.ppermute(piece, "section", onward) for piece in pieces]
    got = {i: exchange(send, i, onward) for i, send in zip(DIRECT, sends)}
    qkv = half_part(pieces[0], mod, w)
    pieces[1], qkv = lax.optimization_barrier((pieces[1], qkv))
    relayed = tuple(i for i in order if i not in DIRECT)
    params = pltpu.CompilerParams(vmem_limit_bytes=LIMIT)
    sends = pick_blocks(pieces, key_blocks, count, relayed, params)
    got.update({i: exchange(send, i, here) for i, send in zip(relayed, sends)})
    x, q, *state = second_part(*pieces, qkv, mod, w)
    early = [arrived_part(count, (EARLY,), x.shape[0] // BLK, *lists_of, [got[EARLY]], mod, w)]
    blocks = [got[i] for i in LATE]
    (out,) = last_part(count, LATE, (), 1, *lists_of, early, blocks, q, state, x, mod, w, wo)
    return out[None]


def solution(mesh):
    return jax.shard_map(
        on_device,
        mesh=mesh,
        in_specs=(
            P("section", "seq", None),
            P("section", None, None),
            P("section", None, None),
            P("section", None, None),
            P(),
            P(),
        ),
        out_specs=P("section", "seq", None),
        check_vma=False,
    )
```

time: 77.8 us -> 71.3 us (0.916)
  the two profiles are of different devices: /device:TPU:0 before, /device:TPU:8 now
where the time goes in v3:
time: 71.3 us; the launch traced here: 71 us
  Pallas kernels  38.1 us (53%)
  starting transfers between devices  15.7 us (22%)
  waiting for transfers between devices  15.1 us (21%)
  local copies, waits for them, and re-layouts  1.88 us (3%)
    pallas_call x2, Pallas kernels, last_part(): pl.pallas_call(functools.partial(last_kernel, count, (EARLY,) * len(early...  16.3 us
    ppermute x8, starting transfers between devices, exchange(): return lax.ppermute(send, ('section', 'seq'), pairs)  14.1 us
    ppermute x2, waiting for transfers between devices, on_device(): pieces = [lax.ppermute(piece, 'section', onward) for piece in pieces]  11.7 us
    pallas_call x1, Pallas kernels, first_part(): pl.pallas_call(first_kernel, out_shape=held[:1] + [state] * 3 + held[1:],...  8.28 us
    pallas_call x2, Pallas kernels, arrived_part(): pl.pallas_call(functools.partial(arrived_kernel, count, exchanges, blocks...  4.55 us
    pallas_call x1, Pallas kernels, second_part(): pl.pallas_call(second_kernel, out_shape=half + [state] * 3, in_specs=[IN_...  3.54 us
    ppermute x8, waiting for transfers between devices, exchange(): return lax.ppermute(send, ('section', 'seq'), pairs)  3.34 us
    pallas_call x2, Pallas kernels, pick_blocks(): pl.pallas_call(functools.partial(pick_kernel, count, exchanges, len(parts...  3.17 us
  transfers between devices with their start and end apart: 10, of which 5 were waited for; matrix products, arithmetic and copies ran while one was open for 0% of the time, Pallas kernels for 27%

profile of v3, /device:TPU:8, one launch (start us, length us, event | category | flops | bytes accessed | tf_op | source)
XLA Modules:
  0.0 71.0 jit_solution(17031300147661573762)
XLA Ops:
  0.0 2.4 %pick_blocks.2 = (bf16[128,1536]{1,0:T(8,128)(2,1)}, bf16[128,1536]{1,0:T(8,128)(2,1)}, bf16[128,1536]{1,0:T(8,128)(2,1)}, bf16[128,1536]{1,0:T(8,128)(2,1)}) custom-call(s32[4,16]{1,0:T(4,128)} %bitcast.20, bf16[256,1536]{1,0:T(8,128)(2,1)} %bitcast.10), custom_call_target="tpu_custom_call" | custom-call | tf_op jit(solution)/shard_map/pick_blocks/pallas_call | solution.py:74
  2.4 3.3 %collective-permute-start = (bf16[128,1536]{1,0:T(8,128)(2,1)}, bf16[128,1536]{1,0:T(8,128)(2,1)S(1)}, u32[]{:S(2)}, u32[]{:S(2)}) collective-permute-start(bf16[128,1536]{1,0:T(8,128)(2,1)} %get-tuple-element.27), channel_id=1, source_target_pairs={{0,0},{1,2},{2,1},{3,4},{4,3},{5,6},{6,5},{7,7},{8,8},{9,10},{10,9... | collective-permute-start | bytes 1179656 | tf_op jit(solution)/shard_map/ppermute | solution.py:374
  5.7 1.7 %collective-permute-start.1 = (bf16[128,1536]{1,0:T(8,128)(2,1)}, bf16[128,1536]{1,0:T(8,128)(2,1)S(1)}, u32[]{:S(2)}, u32[]{:S(2)}) collective-permute-start(bf16[128,1536]{1,0:T(8,128)(2,1)} %get-tuple-element.29), channel_id=1, source_target_pairs={{0,1},{1,0},{2,3},{3,2},{4,5},{5,4},{6,7},{7,6},{8,9},{9,8},{10,11... | collective-permute-start | bytes 1179656 | tf_op jit(solution)/shard_map/ppermute | solution.py:374
  7.4 0.4 collective-permute-start.2
  7.9 3.0 %collective-permute-start.3 = (bf16[128,1536]{1,0:T(8,128)(2,1)}, bf16[128,1536]{1,0:T(8,128)(2,1)S(1)}, u32[]{:S(2)}, u32[]{:S(2)}) collective-permute-start(bf16[128,1536]{1,0:T(8,128)(2,1)} %get-tuple-element.31), channel_id=1, source_target_pairs={{0,0},{1,1},{2,4},{3,5},{4,2},{5,3},{6,6},{7,7},{8,8},{9,9},{10,12... | collective-permute-start | bytes 1179656 | tf_op jit(solution)/shard_map/ppermute | solution.py:374
  10.9 0.0 copy-start
  10.9 1.1 %copy-done = bf16[1,256,1536]{2,1,0:T(8,128)(2,1)S(1)} copy-done((bf16[1,256,1536]{2,1,0:T(8,128)(2,1)S(1)}, bf16[1,256,1536]{2,1,0:T(8,128)(2,1)}, u32[]{:S(2)}) %copy-start) | copy-done | bytes 786456
  12.1 0.0 copy-start.2
  12.1 0.7 %copy-done.2 = f32[1,3,1536]{2,0,1:T(1,128)S(1)} copy-done((f32[1,3,1536]{2,0,1:T(1,128)S(1)}, f32[1,3,1536]{2,0,1:T(1,128)}, u32[]{:S(2)}) %copy-start.2) | copy-done | bytes 18456
  12.8 0.0 copy-start.4
  12.8 0.0 copy-start.5
  12.8 8.3 %first_part.1 = (bf16[256,1536]{1,0:T(8,128)(2,1)S(1)}, f32[256,1536]{1,0:T(8,128)S(1)}, f32[256,1536]{1,0:T(8,128)S(1)}, f32[256,1536]{1,0:T(8,128)S(1)}, bf16[1536,4608]{1,0:T(8,128)(2,1)S(1)}) custom-call(bf16[256,1536]{1,0:T(8,128)(2,1)S(1)} %bitcast.11, f32[3,1,1536]{2,1,0:T(1,128)S(1)} %bitcast.13, bf16[1536,4608]{1,0:T(8,128)(2,1)} %bitcast.26), custom_call_target="tpu_custom_call" | custom-call | tf_op jit(solution)/shard_map/first_part/pallas_call | solution.py:180
  21.1 0.0 collective-permute-done.rest_0_
  21.1 0.0 slice-start
  21.1 0.0 copy-done.4
  21.1 0.0 copy-done.5
  21.1 0.0 slice-start.1
  21.1 0.0 copy-start.1
  21.1 2.3 %arrived_part.2.rest_0_ = bf16[128,3072]{1,0:T(8,128)(2,1)S(1)} custom-call(s32[4,16]{1,0:T(4,128)S(1)} %bitcast.21, s32[16]{0:T(128)S(1)} %copy-done.5, bf16[128,1536]{1,0:T(8,128)(2,1)S(1)} %collective-permute-done.rest_0_, f32[3,1,1536]{2,1,0:T(1,128)S(1)} %bitcast.14, bf16[1536,4608]{1,0:T(8,128)(2,1)S(1)} %get-tuple-element.28.rest_2_.rest_10_.w_ref), custom_call_target="tpu_custom_call" | custom-call | tf_op jit(solution)/shard_map/arrived_part/pallas_call | solution.py:267
  23.4 1.3 %collective-permute-done.1.rest_1_ = bf16[128,1536]{1,0:T(8,128)(2,1)S(1)} collective-permute-done((bf16[128,1536]{1,0:T(8,128)(2,1)}, bf16[128,1536]{1,0:T(8,128)(2,1)S(1)}, u32[]{:S(2)}, u32[]{:S(2)}) %collective-permute-start.1) | collective-permute-done | bytes 393248 | tf_op jit(solution)/shard_map/ppermute | solution.py:374
  24.7 0.0 collective-permute-done.2.rest_2_
  24.7 0.1 collective-permute-done.3.rest_3_
  24.8 0.0 slice-done
  24.8 0.0 slice-done.1
  24.8 0.0 copy-done.1
  24.8 0.0 copy-start.3
  24.8 7.7 %last_part.2 = (bf16[128,1536]{1,0:T(8,128)(2,1)S(1)}, bf16[128,1536]{1,0:T(8,128)(2,1)S(1)}, bf16[128,1536]{1,0:T(8,128)(2,1)S(1)}) custom-call(s32[4,16]{1,0:T(4,128)S(1)} %bitcast.22, s32[16]{0:T(128)S(1)} %copy-done.5, bf16[128,3072]{1,0:T(8,128)(2,1)S(1)} %arrived_part.2.rest_0_, bf16[128,1536]{1,0:T(8,128)(2,1)S(1)} %collective-permute-done.1.rest_1_, ...), custom_call_target="tpu_custom_call" | custom-call | tf_op jit(solution)/shard_map/last_part/pallas_call | solution.py:347
  32.5 0.1 collective-permute-start.5
  32.6 1.6 %collective-permute-start.6 = (bf16[128,1536]{1,0:T(8,128)(2,1)S(1)}, bf16[128,1536]{1,0:T(8,128)(2,1)S(1)}, u32[]{:S(2)}, u32[]{:S(2)}) collective-permute-start(bf16[128,1536]{1,0:T(8,128)(2,1)S(1)} %get-tuple-element.38), channel_id=1, source_target_pairs={{0,8},{8,16},{16,24},{24,0},{1,9},{9,17},{17,25},{25,1},{2,10},{10... | collective-permute-start | bytes 1179656 | tf_op jit(solution)/shard_map/ppermute | solution.py:384
  34.2 0.0 collective-permute-start.4
  34.2 8.1 %collective-permute-done.5.x_ref.refs_0_.a_ref = bf16[128,1536]{1,0:T(8,128)(2,1)S(1)} collective-permute-done((bf16[128,1536]{1,0:T(8,128)(2,1)S(1)}, bf16[128,1536]{1,0:T(8,128)(2,1)S(1)}, u32[]{:S(2)}, u32[]{:S(2)}) %collective-permute-start.5) | collective-permute-done | bytes 393248 | tf_op jit(solution)/shard_map/ppermute | solution.py:384
  42.3 0.0 copy-done.3
  42.3 2.3 %half_part.1.qkv_ref = bf16[128,4608]{1,0:T(8,128)(2,1)S(1)} custom-call(bf16[128,1536]{1,0:T(8,128)(2,1)S(1)} %collective-permute-done.5.x_ref.refs_0_.a_ref, f32[3,1,1536]{2,1,0:T(1,128)S(1)} %bitcast.16, bf16[1536,4608]{1,0:T(8,128)(2,1)S(1)} %get-tuple-element.28.rest_2_.rest_10_.w_ref), custom_call_target="tpu_custom_call" | custom-call | tf_op jit(solution)/shard_map/half_part/pallas_call | solution.py:199
  44.6 3.6 %collective-permute-done.6.refs_1_.b_ref = bf16[128,1536]{1,0:T(8,128)(2,1)S(1)} collective-permute-done((bf16[128,1536]{1,0:T(8,128)(2,1)S(1)}, bf16[128,1536]{1,0:T(8,128)(2,1)S(1)}, u32[]{:S(2)}, u32[]{:S(2)}) %collective-permute-start.6) | collective-permute-done | bytes 393248 | tf_op jit(solution)/shard_map/ppermute | solution.py:384
  48.2 0.7 %pick_blocks.3 = (bf16[128,1536]{1,0:T(8,128)(2,1)S(1)}, bf16[128,1536]{1,0:T(8,128)(2,1)S(1)}, bf16[128,1536]{1,0:T(8,128)(2,1)S(1)}) custom-call(s32[4,16]{1,0:T(4,128)S(1)} %bitcast.23, bf16[128,1536]{1,0:T(8,128)(2,1)S(1)} %collective-permute-done.5.x_ref.refs_0_.a_ref, bf16[128,1536]{1,0:T(8,128)(2,1)S(1)} %collective-permute-done.6.refs_1_.b_ref), custom_call_target="tpu_custom_call" | custom-call | tf_op jit(solution)/shard_map/pick_blocks/pallas_call | solution.py:74
  49.0 0.1 collective-permute-start.7
  49.0 0.5 collective-permute-start.8
  49.5 5.0 %collective-permute-start.9 = (bf16[128,1536]{1,0:T(8,128)(2,1)S(1)}, bf16[128,1536]{1,0:T(8,128)(2,1)S(1)}, u32[]{:S(2)}, u32[]{:S(2)}) collective-permute-start(bf16[128,1536]{1,0:T(8,128)(2,1)S(1)} %get-tuple-element.42), channel_id=1, source_target_pairs={{0,0},{1,1},{2,4},{3,5},{4,2},{5,3},{6,6},{7,7},{8,8},{9,9},{10,12... | collective-permute-start | bytes 1179656 | tf_op jit(solution)/shard_map/ppermute | solution.py:374
  54.5 3.5 %second_part.1 = (bf16[256,1536]{1,0:T(8,128)(2,1)S(1)}, bf16[256,1536]{1,0:T(8,128)(2,1)S(1)}, f32[256,1536]{1,0:T(8,128)S(1)}, f32[256,1536]{1,0:T(8,128)S(1)}, f32[256,1536]{1,0:T(8,128)S(1)}) custom-call(bf16[128,1536]{1,0:T(8,128)(2,1)S(1)} %collective-permute-done.5.x_ref.refs_0_.a_ref, bf16[128,1536]{1,0:T(8,128)(2,1)S(1)} %collective-permute-done.6.refs_1_.b_ref, ...), custom_call_target="tpu_custom_call" | custom-call | tf_op jit(solution)/shard_map/second_part/pallas_call | solution.py:224
  58.1 0.0 collective-permute-done.4.rest_0_
  58.1 2.3 %arrived_part.3.rest_0_ = bf16[128,3072]{1,0:T(8,128)(2,1)S(1)} custom-call(s32[4,16]{1,0:T(4,128)S(1)} %bitcast.24, s32[16]{0:T(128)S(1)} %copy-done.5, bf16[128,1536]{1,0:T(8,128)(2,1)S(1)} %collective-permute-done.4.rest_0_, f32[3,1,1536]{2,1,0:T(1,128)S(1)} %bitcast.18, bf16[1536,4608]{1,0:T(8,128)(2,1)S(1)} %get-tuple-element.28.rest_2_.rest_10_.w_ref), custom_call_target="tpu_custom_call" | custom-call | tf_op jit(solution)/shard_map/arrived_part/pallas_call | solution.py:267
  60.4 0.0 collective-permute-done.7.rest_1_
  60.4 0.0 collective-permute-done.8.rest_2_
  60.4 2.0 %collective-permute-done.9.rest_3_ = bf16[128,1536]{1,0:T(8,128)(2,1)S(1)} collective-permute-done((bf16[128,1536]{1,0:T(8,128)(2,1)S(1)}, bf16[128,1536]{1,0:T(8,128)(2,1)S(1)}, u32[]{:S(2)}, u32[]{:S(2)}) %collective-permute-start.9) | collective-permute-done | bytes 393248 | tf_op jit(solution)/shard_map/ppermute | solution.py:374
  62.4 8.6 %last_part.3 = bf16[256,1536]{1,0:T(8,128)(2,1)} custom-call(s32[4,16]{1,0:T(4,128)S(1)} %bitcast.25, s32[16]{0:T(128)S(1)} %copy-done.5, bf16[128,3072]{1,0:T(8,128)(2,1)S(1)} %arrived_part.3.rest_0_, bf16[128,1536]{1,0:T(8,128)(2,1)S(1)} %collective-permute-done.7.rest_1_, bf16[128,1536]{1,0:T(8,128)(2,1)S(1)} %collective-permute-done.8.rest_2_, ...), custom_call_target="tpu_custom_call" | custom-call | tf_op jit(solution)/shard_map/last_part/pallas_call | solution.py:347
  (1 shorter events, 0.0 us)
Async XLA Ops:
  2.4 18.7 %collective-permute-start = (bf16[128,1536]{1,0:T(8,128)(2,1)}, bf16[128,1536]{1,0:T(8,128)(2,1)S(1)}, u32[]{:S(2)}, u32[]{:S(2)}) collective-permute-start(bf16[128,1536]{1,0:T(8,128)(2,1)} %get-tuple-element.27), channel_id=1, source_target_pairs={{0,0},{1,2},{2,1},{3,4},{4,3},{5,6},{6,5},{7,7},{8,8},{9,10},{10,9... | collective-permute-start | bytes 1179656 | tf_op jit(solution)/shard_map/ppermute | solution.py:374
  5.7 19.0 %collective-permute-start.1 = (bf16[128,1536]{1,0:T(8,128)(2,1)}, bf16[128,1536]{1,0:T(8,128)(2,1)S(1)}, u32[]{:S(2)}, u32[]{:S(2)}) collective-permute-start(bf16[128,1536]{1,0:T(8,128)(2,1)} %get-tuple-element.29), channel_id=1, source_target_pairs={{0,1},{1,0},{2,3},{3,2},{4,5},{5,4},{6,7},{7,6},{8,9},{9,8},{10,11... | collective-permute-start | bytes 1179656 | tf_op jit(solution)/shard_map/ppermute | solution.py:374
  7.4 17.3 %collective-permute-start.2 = (bf16[128,1536]{1,0:T(8,128)(2,1)}, bf16[128,1536]{1,0:T(8,128)(2,1)S(1)}, u32[]{:S(2)}, u32[]{:S(2)}) collective-permute-start(bf16[128,1536]{1,0:T(8,128)(2,1)} %get-tuple-element.30), channel_id=1, source_target_pairs={{0,2},{1,3},{2,0},{3,1},{4,6},{5,7},{6,4},{7,5},{8,10},{9,11},{10,... | collective-permute-start | bytes 1179656 | tf_op jit(solution)/shard_map/ppermute | solution.py:374
  7.9 16.9 %collective-permute-start.3 = (bf16[128,1536]{1,0:T(8,128)(2,1)}, bf16[128,1536]{1,0:T(8,128)(2,1)S(1)}, u32[]{:S(2)}, u32[]{:S(2)}) collective-permute-start(bf16[128,1536]{1,0:T(8,128)(2,1)} %get-tuple-element.31), channel_id=1, source_target_pairs={{0,0},{1,1},{2,4},{3,5},{4,2},{5,3},{6,6},{7,7},{8,8},{9,9},{10,12... | collective-permute-start | bytes 1179656 | tf_op jit(solution)/shard_map/ppermute | solution.py:374
  10.9 1.1 %copy-start = (bf16[1,256,1536]{2,1,0:T(8,128)(2,1)S(1)}, bf16[1,256,1536]{2,1,0:T(8,128)(2,1)}, u32[]{:S(2)}) copy-start(bf16[1,256,1536]{2,1,0:T(8,128)(2,1)} %param.6) | copy-start | bytes 2359300
  12.1 0.7 %copy-start.2 = (f32[1,3,1536]{2,0,1:T(1,128)S(1)}, f32[1,3,1536]{2,0,1:T(1,128)}, u32[]{:S(2)}) copy-start(f32[1,3,1536]{2,0,1:T(1,128)} %param.9) | copy-start | bytes 55300
  12.8 8.3 %copy-start.4 = (s32[16,4]{0,1:T(4,128)S(1)}, s32[16,4]{0,1:T(4,128)}, u32[]{:S(2)}) copy-start(s32[16,4]{0,1:T(4,128)} %param.10) | copy-start | bytes 772
  12.8 8.3 %copy-start.5 = (s32[16]{0:T(128)S(1)}, s32[16]{0:T(128)}, u32[]{:S(2)}) copy-start(s32[16]{0:T(128)} %count_ref.7) | copy-start | bytes 196
  21.1 3.7 %slice-start = ((s8[4718592]{0:T(1024)(128)(4,1)}), s8[4194304]{0:T(1024)(128)(4,1)S(1)}, s32[]{:S(2)}) async-start(s8[4718592]{0:T(1024)(128)(4,1)} %bitcast.6), calls=%async_computation | async-start | bytes 8388608
  21.1 3.7 %slice-start.1 = ((s8[4718592]{0:T(1024)(128)(4,1)}), s8[524288]{0:T(1024)(128)(4,1)S(1)}, s32[]{:S(2)}) async-start(s8[4718592]{0:T(1024)(128)(4,1)} %bitcast.6), calls=%async_computation.1 | async-start | bytes 1048576
  21.1 3.7 %copy-start.1 = (bf16[1,256,1536]{2,1,0:T(8,128)(2,1)S(1)}, bf16[1,256,1536]{2,1,0:T(8,128)(2,1)}, u32[]{:S(2)}) copy-start(bf16[1,256,1536]{2,1,0:T(8,128)(2,1)} %param.6) | copy-start | bytes 2359300
  24.8 17.5 %copy-start.3 = (f32[1,3,1536]{2,0,1:T(1,128)S(1)}, f32[1,3,1536]{2,0,1:T(1,128)}, u32[]{:S(2)}) copy-start(f32[1,3,1536]{2,0,1:T(1,128)} %param.9) | copy-start | bytes 55300
  32.5 9.8 %collective-permute-start.5 = (bf16[128,1536]{1,0:T(8,128)(2,1)S(1)}, bf16[128,1536]{1,0:T(8,128)(2,1)S(1)}, u32[]{:S(2)}, u32[]{:S(2)}) collective-permute-start(bf16[128,1536]{1,0:T(8,128)(2,1)S(1)} %get-tuple-element.37), channel_id=1, source_target_pairs={{0,8},{8,16},{16,24},{24,0},{1,9},{9,17},{17,25},{25,1},{2,10},{10... | collective-permute-start | bytes 1179656 | tf_op jit(solution)/shard_map/ppermute | solution.py:384
  32.6 15.6 %collective-permute-start.6 = (bf16[128,1536]{1,0:T(8,128)(2,1)S(1)}, bf16[128,1536]{1,0:T(8,128)(2,1)S(1)}, u32[]{:S(2)}, u32[]{:S(2)}) collective-permute-start(bf16[128,1536]{1,0:T(8,128)(2,1)S(1)} %get-tuple-element.38), channel_id=1, source_target_pairs={{0,8},{8,16},{16,24},{24,0},{1,9},{9,17},{17,25},{25,1},{2,10},{10... | collective-permute-start | bytes 1179656 | tf_op jit(solution)/shard_map/ppermute | solution.py:384
  34.2 23.9 %collective-permute-start.4 = (bf16[128,1536]{1,0:T(8,128)(2,1)S(1)}, bf16[128,1536]{1,0:T(8,128)(2,1)S(1)}, u32[]{:S(2)}, u32[]{:S(2)}) collective-permute-start(bf16[128,1536]{1,0:T(8,128)(2,1)S(1)} %get-tuple-element.36), channel_id=1, source_target_pairs={{0,8},{1,10},{2,9},{3,12},{4,11},{5,14},{6,13},{7,15},{8,16},{9,18... | collective-permute-start | bytes 1179656 | tf_op jit(solution)/shard_map/ppermute | solution.py:374
  49.0 11.4 %collective-permute-start.7 = (bf16[128,1536]{1,0:T(8,128)(2,1)S(1)}, bf16[128,1536]{1,0:T(8,128)(2,1)S(1)}, u32[]{:S(2)}, u32[]{:S(2)}) collective-permute-start(bf16[128,1536]{1,0:T(8,128)(2,1)S(1)} %get-tuple-element.40), channel_id=1, source_target_pairs={{0,1},{1,0},{2,3},{3,2},{4,5},{5,4},{6,7},{7,6},{8,9},{9,8},{10,11... | collective-permute-start | bytes 1179656 | tf_op jit(solution)/shard_map/ppermute | solution.py:374
  49.0 11.4 %collective-permute-start.8 = (bf16[128,1536]{1,0:T(8,128)(2,1)S(1)}, bf16[128,1536]{1,0:T(8,128)(2,1)S(1)}, u32[]{:S(2)}, u32[]{:S(2)}) collective-permute-start(bf16[128,1536]{1,0:T(8,128)(2,1)S(1)} %get-tuple-element.41), channel_id=1, source_target_pairs={{0,2},{1,3},{2,0},{3,1},{4,6},{5,7},{6,4},{7,5},{8,10},{9,11},{10,... | collective-permute-start | bytes 1179656 | tf_op jit(solution)/shard_map/ppermute | solution.py:374
  49.5 12.9 %collective-permute-start.9 = (bf16[128,1536]{1,0:T(8,128)(2,1)S(1)}, bf16[128,1536]{1,0:T(8,128)(2,1)S(1)}, u32[]{:S(2)}, u32[]{:S(2)}) collective-permute-start(bf16[128,1536]{1,0:T(8,128)(2,1)S(1)} %get-tuple-element.42), channel_id=1, source_target_pairs={{0,0},{1,1},{2,4},{3,5},{4,2},{5,3},{6,6},{7,7},{8,8},{9,9},{10,12... | collective-permute-start | bytes 1179656 | tf_op jit(solution)/shard_map/ppermute | solution.py:374
